TPU v7x, 512 devices: a whole 4x8x8 slice. The times are simulated.
512 devices in a mesh: blk: 2 (over core), ctx: 32 (over y, x), tp: 8 (over z).
Axes of the slice: x: 4, y: 8, z: 8, core: 2. Of those that a mesh axis runs over, the one named last changes fastest.
Arguments:
- queries: bfloat16 [8192, 5120], P(('blk', 'ctx'), 'tp'), may hold values from -5 to 5
- keys: bfloat16 [8192, 5120], P(('blk', 'ctx'), 'tp'), may hold values from -5 to 5
- values: bfloat16 [8192, 5120], P(('blk', 'ctx'), 'tp'), may hold values from -6 to 6
- lengths: int32 [32], replicated, may hold values from 1 to 5120, 8192 in all
Outputs:
- attended: bfloat16 [8192, 5120], P(('blk', 'ctx'), 'tp')
Inputs may be any that keep to these rules, and one draw needn't show every extreme that they name: The lengths sum to 8192.
All inputs are finite; a program needn't handle non-finite values.
Results may differ from a plain program's by a relative error of at most 0.006.
Values may be sent and summed in bfloat16 or wider, within the bound.
No kernel may reach another device: no remote copies, remote signals or barrier semaphores. Data moves between devices by JAX's collectives and lax.ppermute only.
A program may use at most 64 MiB of HBM per device.

v0:
```python
import functools
import math

import jax
import jax.numpy as jnp
from jax import lax
from jax.experimental import pallas as pl
from jax.experimental.pallas import tpu as pltpu
from jax.sharding import Mesh, PartitionSpec as P

HEAD_DIM = 128
ROWS = 128
X = 4
Y = 8
HEADS = 5
DOCS = 32
SPAN = X * ROWS
WIDE = 2 * SPAN
WIDE_SHIFT = 10
TILE = 4 * ROWS
HALF = TILE // 2
TILES = Y // 2
GROUP = Y * SPAN
STATS = 16
NEG = -1e30
LOG2E = math.log2(math.e)
C = LOG2E / math.sqrt(HEAD_DIM)
KEY_PAIRS = [(x, X - 1 - x) for x in range(X)]
QUERY_PAIRS = [(0, 1), (1, 0)]


def pack_kernel(q_ref, k_ref, v_ref, out_ref):
    for h in range(HEADS):
        cols = slice(h * HEAD_DIM, (h + 1) * HEAD_DIM)
        out_ref[h, :ROWS, :] = q_ref[:, cols].T
        out_ref[h, ROWS : 2 * ROWS, :] = k_ref[:, cols]
        out_ref[h, 2 * ROWS :, :] = v_ref[:, cols].T


def pack(q, k, v):
    return pl.pallas_call(
        pack_kernel,
        out_shape=jax.ShapeDtypeStruct((Y, 2 * ROWS + HEAD_DIM, HEAD_DIM), jnp.bfloat16),
        name="pack",
    )(q, k, v)


def combine_kernel(in_ref, out_ref):
    logs = []
    for h in range(HEADS):
        for n in range(2):
            terms = in_ref[h, n, ROWS:, :].astype(jnp.float32)
            logs.append(terms[0:1] + terms[1:2] + terms[2:3])
    a = jnp.concatenate(logs[::2] + logs[:1] * (8 - HEADS), axis=0)
    b = jnp.concatenate(logs[1::2] + logs[1:2] * (8 - HEADS), axis=0)
    top = jnp.maximum(a, b)
    a, b = jnp.exp2(a - top), jnp.exp2(b - top)
    total = a + b
    shares = jnp.concatenate([a / total, b / total], axis=0).T
    for h in range(HEADS):
        a = in_ref[h, 0, :ROWS, :].astype(jnp.float32) * shares[:, h : h + 1]
        b = in_ref[h, 1, :ROWS, :].astype(jnp.float32) * shares[:, 8 + h : 9 + h]
        out_ref[:, h * HEAD_DIM : (h + 1) * HEAD_DIM] = (a + b).astype(jnp.bfloat16)


def combine(parts):
    return pl.pallas_call(
        combine_kernel,
        out_shape=jax.ShapeDtypeStruct((ROWS, HEADS * HEAD_DIM), jnp.bfloat16),
        name="combine",
    )(parts)


def places(x, shape):
    n = lax.broadcasted_iota(jnp.int32, shape, 1)
    return (
        jnp.where(n < 2 * ROWS, x, x ^ 1) * ROWS
        + (lax.shift_right_logical(n, 7) & 1) * SPAN
        + (n & (ROWS - 1))
    )


def find_documents(blk, x, len_ref, first_ref, lo_ref, hi_ref):
    base = blk * GROUP
    pos = places(x, (8, TILE)) + lax.broadcasted_iota(jnp.int32, (8, TILE), 0) * WIDE
    lowest = jnp.minimum(x, x ^ 1) * ROWS
    highest = SPAN + jnp.maximum(x, x ^ 1) * ROWS + ROWS - 1
    start = -base
    first = jnp.zeros((8, TILE), jnp.int32) - base
    los = [start] * TILES
    his = [start] * TILES
    for j in range(DOCS - 1):
        start = start + len_ref[j]
        first = jnp.where(pos >= start, start, first)
        los = [jnp.where(lowest + i * WIDE >= start, start, los[i]) for i in range(TILES)]
        his = [jnp.where(highest + i * WIDE >= start, start, his[i]) for i in range(TILES)]
    first_ref[...] = first
    for i in range(TILES):
        lo_ref[i] = lax.shift_right_arithmetic(los[i], WIDE_SHIFT)
        hi_ref[i] = lax.shift_right_arithmetic(his[i], WIDE_SHIFT)


def load_block(own_ref, pair_ref, k_ref, vt_ref, j):
    for n, ref in enumerate((own_ref, pair_ref, own_ref, pair_ref)):
        y = 2 * j + n // 2
        part = slice(n * ROWS, (n + 1) * ROWS)
        k_ref[j, part, :] = ref[y, :ROWS, :]
        vt_ref[j, :, part] = ref[y, ROWS:, :]


def key_places(x):
    row = lax.broadcasted_iota(jnp.int32, (HALF, TILE), 0)
    return jnp.where(row < ROWS, x, X - 1 - x) * ROWS + (row & (ROWS - 1))


def load_queries(q_own_ref, q_pair_ref, i):
    return jnp.concatenate(
        [q_own_ref[2 * i], q_own_ref[2 * i + 1], q_pair_ref[2 * i], q_pair_ref[2 * i + 1]],
        axis=1,
    )


def scores_of(k_ref, s_ref, q, g, n, m, kept):
    part = slice(n * HALF, (n + 1) * HALF)
    s = jnp.dot(k_ref[g, part, :], q, preferred_element_type=jnp.float32)
    if kept is not None:
        s = jnp.where(kept, s, NEG)
    s_ref[g, part, :] = s
    return jnp.maximum(m, jnp.max(s.reshape(HALF // 8, 8, TILE), axis=0))


def mix(vt_ref, s_ref, g, n, shift, l, acc):
    part = slice(n * HALF, (n + 1) * HALF)
    p = jnp.exp2(s_ref[g, part, :] * C - shift)
    l = l + jnp.sum(p.reshape(HALF // 8, 8, TILE), axis=0)
    acc = acc + jnp.dot(
        vt_ref[g, :, part], p.astype(jnp.bfloat16), preferred_element_type=jnp.float32
    )
    return l, acc


def mix_block(vt_ref, s_ref, g, shift, l, acc):
    for n in range(2):
        l, acc = mix(vt_ref, s_ref, g, n, shift, l, acc)
    return l, acc


def shift_of(top):
    return jnp.where(top > 0.5 * NEG, top * C, 0.0)


def own_kernel(
    place_ref,
    len_ref,
    q_own_ref,
    q_pair_ref,
    own_ref,
    pair_ref,
    acc_ref,
    state_ref,
    first_ref,
    lo_ref,
    hi_ref,
    k_ref,
    vt_ref,
    even_ref,
    odd_ref,
):
    blk, x, slot = place_ref[0], place_ref[1], place_ref[2]

    @pl.when(slot < HEADS)
    def _():
        find_documents(blk, x, len_ref, first_ref, lo_ref, hi_ref)

        def load(j, _):
            load_block(own_ref, pair_ref, k_ref, vt_ref, j)
            return 0

        lax.fori_loop(0, TILES, load, 0)
        key_rows = key_places(x)

        def score(s_ref, i, q, g, n, m, masked, diagonal):
            kept = None
            if masked:
                kept = key_rows >= first_ref[i : i + 1, :] - (g * WIDE + n * SPAN)
                if diagonal:
                    kept &= key_rows <= places(x, (1, TILE)) - n * SPAN
            return scores_of(k_ref, s_ref, q, g, n, m, kept)

        def score_diagonal(s_ref, i, q, m):
            for n in range(2):
                m = score(s_ref, i, q, i, n, m, True, True)
            return m

        none = jnp.full((8, TILE), NEG, jnp.float32)
        zeros = jnp.zeros((8, TILE), jnp.float32)
        buffers = (even_ref, odd_ref)
        q = load_queries(q_own_ref, q_pair_ref, 0)
        m = score_diagonal(even_ref, 0, q, none)
        for i in range(TILES):
            s_ref, later_ref = buffers[i % 2], buffers[(i + 1) % 2]
            top = jnp.max(m, axis=0, keepdims=True)
            shift = shift_of(top)
            begin = jnp.maximum(lo_ref[i], 0)
            sums = (zeros, jnp.zeros((HEAD_DIM, TILE), jnp.float32))
            if i + 1 < TILES:
                q = load_queries(q_own_ref, q_pair_ref, i + 1)

                def step(masked, g, carry, i=i, q=q, shift=shift, s_ref=s_ref, later_ref=later_ref):
                    m, l, acc = carry
                    for n in range(2):
                        l, acc = mix(vt_ref, s_ref, g, n, shift, l, acc)
                        m = score(later_ref, i + 1, q, g, n, m, masked, False)
                    return m, l, acc

                carry = (none,) + sums
                if i > 0:
                    middle = jnp.clip(hi_ref[i + 1] + 1, begin, i)
                    carry = lax.fori_loop(begin, middle, functools.partial(step, True), carry)
                    carry = lax.fori_loop(middle, i, functools.partial(step, False), carry)
                m, l, acc = step(True, i, carry)
                m = score_diagonal(later_ref, i + 1, q, m)
            else:
                l, acc = lax.fori_loop(
                    begin,
                    i + 1,
                    lambda g, c, s_ref=s_ref, shift=shift: mix_block(vt_ref, s_ref, g, shift, *c),
                    sums,
                )
            l = jnp.sum(l, axis=0, keepdims=True)
            row = lax.broadcasted_iota(jnp.int32, (8, TILE), 0)
            acc_ref[i] = acc
            state_ref[i] = jnp.where(row == 0, l, top)


def prev_kernel(
    place_ref,
    len_ref,
    q_own_ref,
    q_pair_ref,
    prev_own_ref,
    prev_pair_ref,
    acc_ref,
    state_ref,
    o_ref,
    first_ref,
    lo_ref,
    hi_ref,
    k_ref,
    vt_ref,
    even_ref,
    odd_ref,
):
    blk, x, slot = place_ref[0], place_ref[1], place_ref[2]

    @pl.when(slot < HEADS)
    def _():
        find_documents(blk, x, len_ref, first_ref, lo_ref, hi_ref)

        def begin_of(i):
            return jnp.where(blk > 0, jnp.clip(lo_ref[i] + TILES, 0, TILES), TILES)

        def load(j, _):
            load_block(prev_own_ref, prev_pair_ref, k_ref, vt_ref, j)
            return 0

        lax.fori_loop(begin_of(0), TILES, load, 0)
        key_rows = key_places(x)

        def score(s_ref, i, q, g, n, m, masked):
            kept = None
            if masked:
                kept = key_rows >= first_ref[i : i + 1, :] - ((g - TILES) * WIDE + n * SPAN)
            return scores_of(k_ref, s_ref, q, g, n, m, kept)

        def score_first(masked, g, m):
            for n in range(2):
                m = score(even_ref, 0, q, g, n, m, masked)
            return m

        def middle_of(i, begin):
            return jnp.clip(hi_ref[i] + TILES + 1, begin, TILES)

        none = jnp.full((8, TILE), NEG, jnp.float32)
        zeros = jnp.zeros((8, TILE), jnp.float32)
        buffers = (even_ref, odd_ref)
        q = load_queries(q_own_ref, q_pair_ref, 0)
        begin = begin_of(0)
        middle = middle_of(0, begin)
        m = lax.fori_loop(begin, middle, functools.partial(score_first, True), none)
        m = lax.fori_loop(middle, TILES, functools.partial(score_first, False), m)
        for i in range(TILES):
            s_ref, later_ref = buffers[i % 2], buffers[(i + 1) % 2]
            own_l, own_top = state_ref[i, 0:1, :], state_ref[i, 1:2, :]
            top = jnp.maximum(jnp.max(m, axis=0, keepdims=True), own_top)
            shift = shift_of(top)
            scale = jnp.where(own_top > 0.5 * NEG, jnp.exp2(own_top * C - shift), 0.0)
            begin = begin_of(i)
            sums = (zeros, acc_ref[i] * scale)
            if i + 1 < TILES:
                q = load_queries(q_own_ref, q_pair_ref, i + 1)

                def step(masked, g, carry, i=i, q=q, shift=shift, s_ref=s_ref, later_ref=later_ref):
                    m, l, acc = carry
                    for n in range(2):
                        l, acc = mix(vt_ref, s_ref, g, n, shift, l, acc)
                        m = score(later_ref, i + 1, q, g, n, m, masked)
                    return m, l, acc

                middle = middle_of(i + 1, begin)
                carry = (none,) + sums
                carry = lax.fori_loop(begin, middle, functools.partial(step, True), carry)
                m, l, acc = lax.fori_loop(middle, TILES, functools.partial(step, False), carry)
            else:
                l, acc = lax.fori_loop(
                    begin,
                    TILES,
                    lambda g, c, s_ref=s_ref, shift=shift: mix_block(vt_ref, s_ref, g, shift, *c),
                    sums,
                )
            l = jnp.sum(l, axis=0, keepdims=True) + own_l * scale
            some = l > 0.0
            l = jnp.where(some, l, 1.0)
            o = acc / l
            log = jnp.where(some, shift + jnp.log(l) * LOG2E, NEG)
            high = log.astype(jnp.bfloat16).astype(jnp.float32)
            middle = (log - high).astype(jnp.bfloat16).astype(jnp.float32)
            low = log - high - middle
            row = lax.broadcasted_iota(jnp.int32, (STATS, TILE), 0)
            stats = jnp.where(row == 0, high, jnp.where(row == 1, middle, low))
            stats = stats.astype(jnp.bfloat16)
            for n in range(4):
                part = slice(n * ROWS, (n + 1) * ROWS)
                y, to = 2 * i + (n & 1), (x & 1) ^ (n >> 1)
                o_ref[y, to, :ROWS, :] = o[:, part].T.astype(jnp.bfloat16)
                o_ref[y, to, ROWS:, :] = stats[:, part]


SCRATCH = [
    pltpu.VMEM((8, TILE), jnp.int32),
    pltpu.SMEM((TILES,), jnp.int32),
    pltpu.SMEM((TILES,), jnp.int32),
    pltpu.VMEM((TILES, TILE, HEAD_DIM), jnp.bfloat16),
    pltpu.VMEM((TILES, HEAD_DIM, TILE), jnp.bfloat16),
    pltpu.VMEM((TILES, TILE, TILE), jnp.float32),
    pltpu.VMEM((TILES, TILE, TILE), jnp.float32),
]
SMEM = pl.BlockSpec(memory_space=pltpu.SMEM)
VMEM = pl.BlockSpec(memory_space=pltpu.VMEM)
ACC = (TILES, HEAD_DIM, TILE)


def attend_own(place, lengths, q_own, q_pair, own, pair):
    return pl.pallas_call(
        own_kernel,
        out_shape=(
            jax.ShapeDtypeStruct(ACC, jnp.float32),
            jax.ShapeDtypeStruct((TILES, 8, TILE), jnp.float32),
        ),
        in_specs=[SMEM, SMEM] + [VMEM] * 4,
        out_specs=(VMEM, VMEM),
        scratch_shapes=SCRATCH,
        compiler_params=pltpu.CompilerParams(vmem_limit_bytes=20 << 20),
        cost_estimate=pl.CostEstimate(
            flops=1 << 30, bytes_accessed=4 << 20, transcendentals=2 << 20
        ),
        name="attend_own",
    )(place, lengths, q_own, q_pair, own, pair)


def attend_prev(place, lengths, q_own, q_pair, prev_own, prev_pair, acc, state):
    return pl.pallas_call(
        prev_kernel,
        out_shape=jax.ShapeDtypeStruct((Y, 2, ROWS + STATS, HEAD_DIM), jnp.bfloat16),
        in_specs=[SMEM, SMEM] + [VMEM] * 6,
        out_specs=VMEM,
        scratch_shapes=SCRATCH,
        compiler_params=pltpu.CompilerParams(vmem_limit_bytes=20 << 20),
        cost_estimate=pl.CostEstimate(
            flops=1 << 29, bytes_accessed=4 << 20, transcendentals=1 << 20
        ),
        name="attend_prev",
    )(place, lengths, q_own, q_pair, prev_own, prev_pair, acc, state)


def body(queries, keys, values, lengths):
    x = 2 * lax.axis_index("xh") + lax.axis_index("xl")
    place = jnp.stack([lax.axis_index("blk"), x, lax.axis_index("y")]).astype(jnp.int32)
    got = lax.all_to_all(pack(queries, keys, values), "y", 0, 0, tiled=True)
    own_queries, own = got[:, :ROWS], got[:, ROWS:]
    pair = lax.ppermute(own, ("xh", "xl"), KEY_PAIRS)
    pair_queries = lax.ppermute(own_queries, "xl", QUERY_PAIRS)
    prev_own = lax.ppermute(own, "blk", [(0, 1)])
    pair, pair_queries = lax.optimization_barrier((pair, pair_queries))
    prev_pair = lax.ppermute(pair, "blk", [(0, 1)])
    state = attend_own(place, lengths, own_queries, pair_queries, own, pair)
    parts = attend_prev(place, lengths, own_queries, pair_queries, prev_own, prev_pair, *state)
    parts = parts.reshape(2 * Y, ROWS + STATS, HEAD_DIM)
    parts = lax.all_to_all(parts, ("y", "xl"), 0, 0, tiled=True)
    return combine(parts.reshape(Y, 2, ROWS + STATS, HEAD_DIM))


def solution(mesh):
    devices = mesh.devices.reshape(2, Y, 2, 2, mesh.devices.shape[2])
    fine = Mesh(devices, ("blk", "y", "xh", "xl", "tp"))
    rows = P(("blk", "y", "xh", "xl"), "tp")
    return jax.shard_map(
        body, mesh=fine, in_specs=(rows, rows, rows, P()), out_specs=rows, check_vma=False
    )
```

profile of v0, /device:TPU:1, one launch (start us, length us, event | category | flops | bytes accessed | tf_op | source)
XLA Modules:
  0.0 83.2 jit_solution(1060373005051602986)
XLA Ops:
  0.0 2.1 %pack.1 = bf16[8,384,128]{2,1,0:T(8,128)(2,1)} custom-call(bf16[128,640]{1,0:T(8,128)(2,1)} %q_ref.1, bf16[128,640]{1,0:T(8,128)(2,1)} %k_ref.1, bf16[128,640]{1,0:T(8,128)(2,1)} %v_ref.1), custom_call_target="tpu_custom_call" | custom-call | tf_op jit(solution)/shard_map/pack/pallas_call | solution.py:41
  2.1 27.6 %all_to_all.10 = bf16[8,384,128]{2,1,0:T(8,128)(2,1)S(1)} all-to-all(bf16[8,384,128]{2,1,0:T(8,128)(2,1)} %pack.1), channel_id=1, replica_groups=mesh['blk'=2,'y'=8,'xh'=2,'xl'=2,'tp'=8] {'y'}, dimensions={0} | all-to-all | bytes 1572864 | tf_op jit(solution)/shard_map/all_to_all | solution.py:389
  29.8 6.0 %collective-permute-start = (bf16[8,256,128]{2,1,0:T(8,128)(2,1)S(1)}, bf16[8,256,128]{2,1,0:T(8,128)(2,1)S(1)}, u32[]{:S(2)}, u32[]{:S(2)}) collective-permute-start(bf16[8,256,128]{2,1,0:T(8,128)(2,1)S(1)} %slice.9.own_ref), channel_id=1, source_target_pairs={{0,24},{8,16},{16,8},{24,0},{1,25},{9,17},{17,9},{25,1},{2,26},{10... | collective-permute-start | bytes 1572872 | tf_op jit(solution)/shard_map/ppermute | solution.py:391
  35.8 1.9 %collective-permute-start.1 = (bf16[8,128,128]{2,1,0:T(8,128)(2,1)S(1)}, bf16[8,128,128]{2,1,0:T(8,128)(2,1)S(1)}, u32[]{:S(2)}, u32[]{:S(2)}) collective-permute-start(bf16[8,128,128]{2,1,0:T(8,128)(2,1)S(1)} %slice.8.q_own_ref), channel_id=1, source_target_pairs={{0,8},{8,0},{1,9},{9,1},{2,10},{10,2},{3,11},{11,3},{4,12},{12,4},... | collective-permute-start | bytes 786440 | tf_op jit(solution)/shard_map/ppermute | solution.py:392
  37.8 1.3 %collective-permute-start.2 = (bf16[8,256,128]{2,1,0:T(8,128)(2,1)S(1)}, bf16[8,256,128]{2,1,0:T(8,128)(2,1)S(1)}, u32[]{:S(2)}, u32[]{:S(2)}) collective-permute-start(bf16[8,256,128]{2,1,0:T(8,128)(2,1)S(1)} %slice.9.own_ref), channel_id=1, source_target_pairs={{0,256},{1,257},{2,258},{3,259},{4,260},{5,261},{6,262},{7,263},{8... | collective-permute-start | bytes 1572872 | tf_op jit(solution)/shard_map/ppermute | solution.py:393
  39.1 4.2 %collective-permute-done.1.q_pair_ref = bf16[8,128,128]{2,1,0:T(8,128)(2,1)S(1)} collective-permute-done((bf16[8,128,128]{2,1,0:T(8,128)(2,1)S(1)}, bf16[8,128,128]{2,1,0:T(8,128)(2,1)S(1)}, u32[]{:S(2)}, u32[]{:S(2)}) %collective-permute-start.1) | collective-permute-done | bytes 262176 | tf_op jit(solution)/shard_map/ppermute | solution.py:392
  43.2 1.9 %collective-permute-done.pair_ref = bf16[8,256,128]{2,1,0:T(8,128)(2,1)S(1)} collective-permute-done((bf16[8,256,128]{2,1,0:T(8,128)(2,1)S(1)}, bf16[8,256,128]{2,1,0:T(8,128)(2,1)S(1)}, u32[]{:S(2)}, u32[]{:S(2)}) %collective-permute-start) | collective-permute-done | bytes 524320 | tf_op jit(solution)/shard_map/ppermute | solution.py:391
  45.1 1.3 %collective-permute-start.3 = (bf16[8,256,128]{2,1,0:T(8,128)(2,1)S(1)}, bf16[8,256,128]{2,1,0:T(8,128)(2,1)S(1)}, u32[]{:S(2)}, u32[]{:S(2)}) collective-permute-start(bf16[8,256,128]{2,1,0:T(8,128)(2,1)S(1)} %collective-permute-done.pair_ref), channel_id=1, source_target_pairs={{0,256},{1,257},{2,258},{3,259},{4,260},{5,261},{6,262},{7,263},{8... | collective-permute-start | bytes 1572872 | tf_op jit(solution)/shard_map/ppermute | solution.py:395
  46.4 0.0 copy-start
  46.4 0.1 pad_add_fusion.place_ref
  46.5 0.6 copy-done
  47.1 5.4 %attend_own.1 = (f32[4,128,512]{2,1,0:T(8,128)S(1)}, f32[4,8,512]{2,1,0:T(8,128)S(1)}) custom-call(s32[3]{0:T(128)S(1)} %pad_add_fusion.place_ref, s32[32]{0:T(128)S(1)} %copy-done, bf16[8,128,128]{2,1,0:T(8,128)(2,1)S(1)} %slice.8.q_own_ref, bf16[8,128,128]{2,1,0:T(8,128)(2,1)S(1)} %collective-permute-done.1.q_pair_ref, ...), custom_call_target="tpu_custom_call" | custom-call | flops 1073741824 | bytes 4194304 | tf_op jit(solution)/shard_map/attend_own/pallas_call | solution.py:354
  52.4 0.0 collective-permute-done.2.prev_own_ref
  52.4 0.0 collective-permute-done.3.prev_pair_ref
  52.5 6.6 %attend_prev.1 = bf16[8,2,144,128]{3,2,1,0:T(8,128)(2,1)S(1)} custom-call(s32[3]{0:T(128)S(1)} %pad_add_fusion.place_ref, s32[32]{0:T(128)S(1)} %copy-done, bf16[8,128,128]{2,1,0:T(8,128)(2,1)S(1)} %slice.8.q_own_ref, bf16[8,128,128]{2,1,0:T(8,128)(2,1)S(1)} %collective-permute-done.1.q_pair_ref, ...), custom_call_target="tpu_custom_call" | custom-call | flops 536870912 | bytes 4194304 | tf_op jit(solution)/shard_map/attend_prev/pallas_call | solution.py:372
  59.1 22.0 %all_to_all.11 = bf16[16,144,128]{2,1,0:T(8,128)(2,1)} all-to-all(bf16[16,144,128]{2,1,0:T(8,128)(2,1)S(1)} %bitcast.5), channel_id=1, replica_groups=mesh['blk'=2,'y'=8,'xh'=2,'xl'=2,'tp'=8] {'y','xl'}, dimensions={0} | all-to-all | bytes 1179648 | tf_op jit(solution)/shard_map/all_to_all | solution.py:399
  81.1 2.1 %combine.1 = bf16[128,640]{1,0:T(8,128)(2,1)} custom-call(bf16[8,2,144,128]{3,2,1,0:T(8,128)(2,1)} %bitcast.6), custom_call_target="tpu_custom_call" | custom-call | tf_op jit(solution)/shard_map/combine/pallas_call | solution.py:67
  (2 shorter events, 0.1 us)
Async XLA Ops:
  29.8 15.3 %collective-permute-start = (bf16[8,256,128]{2,1,0:T(8,128)(2,1)S(1)}, bf16[8,256,128]{2,1,0:T(8,128)(2,1)S(1)}, u32[]{:S(2)}, u32[]{:S(2)}) collective-permute-start(bf16[8,256,128]{2,1,0:T(8,128)(2,1)S(1)} %slice.9.own_ref), channel_id=1, source_target_pairs={{0,24},{8,16},{16,8},{24,0},{1,25},{9,17},{17,9},{25,1},{2,26},{10... | collective-permute-start | bytes 1572872 | tf_op jit(solution)/shard_map/ppermute | solution.py:391
  35.8 7.4 %collective-permute-start.1 = (bf16[8,128,128]{2,1,0:T(8,128)(2,1)S(1)}, bf16[8,128,128]{2,1,0:T(8,128)(2,1)S(1)}, u32[]{:S(2)}, u32[]{:S(2)}) collective-permute-start(bf16[8,128,128]{2,1,0:T(8,128)(2,1)S(1)} %slice.8.q_own_ref), channel_id=1, source_target_pairs={{0,8},{8,0},{1,9},{9,1},{2,10},{10,2},{3,11},{11,3},{4,12},{12,4},... | collective-permute-start | bytes 786440 | tf_op jit(solution)/shard_map/ppermute | solution.py:392
  37.8 14.7 %collective-permute-start.2 = (bf16[8,256,128]{2,1,0:T(8,128)(2,1)S(1)}, bf16[8,256,128]{2,1,0:T(8,128)(2,1)S(1)}, u32[]{:S(2)}, u32[]{:S(2)}) collective-permute-start(bf16[8,256,128]{2,1,0:T(8,128)(2,1)S(1)} %slice.9.own_ref), channel_id=1, source_target_pairs={{0,256},{1,257},{2,258},{3,259},{4,260},{5,261},{6,262},{7,263},{8... | collective-permute-start | bytes 1572872 | tf_op jit(solution)/shard_map/ppermute | solution.py:393
  45.1 7.3 %collective-permute-start.3 = (bf16[8,256,128]{2,1,0:T(8,128)(2,1)S(1)}, bf16[8,256,128]{2,1,0:T(8,128)(2,1)S(1)}, u32[]{:S(2)}, u32[]{:S(2)}) collective-permute-start(bf16[8,256,128]{2,1,0:T(8,128)(2,1)S(1)} %collective-permute-done.pair_ref), channel_id=1, source_target_pairs={{0,256},{1,257},{2,258},{3,259},{4,260},{5,261},{6,262},{7,263},{8... | collective-permute-start | bytes 1572872 | tf_op jit(solution)/shard_map/ppermute | solution.py:395
  46.4 0.7 copy-start
where the time goes:
time: 83.6 us; the launch traced here: 83.2 us
  blocking collectives  49.6 us (59%)
  Pallas kernels  16.2 us (19%)
  starting transfers between devices  10.5 us (13%)
  waiting for transfers between devices  6.05 us (7%)
    all_to_all x1, blocking collectives, body(): got = lax.all_to_all(pack(queries, keys, values), 'y', 0, 0, tiled=True)  27.6 us
    all_to_all x1, blocking collectives, body(): parts = lax.all_to_all(parts, ('y', 'xl'), 0, 0, tiled=True)  22 us
    pallas_call x1, Pallas kernels, attend_prev(): pl.pallas_call(prev_kernel, out_shape=jax.ShapeDtypeStruct((Y, 2, ROWS +...  6.61 us
    ppermute x1, starting transfers between devices, body(): pair = lax.ppermute(own, ('xh', 'xl'), KEY_PAIRS)  6.03 us
    pallas_call x1, Pallas kernels, attend_own(): pl.pallas_call(own_kernel, out_shape=(jax.ShapeDtypeStruct(ACC, jnp.float...  5.37 us
    ppermute x1, waiting for transfers between devices, body(): pair_queries = lax.ppermute(own_queries, 'xl', QUERY_PAIRS)  4.18 us
    pallas_call x1, Pallas kernels, combine(): pl.pallas_call(combine_kernel, out_shape=jax.ShapeDtypeStruct((ROWS, HEAD...  2.13 us
    pallas_call x1, Pallas kernels, pack(): pl.pallas_call(pack_kernel, out_shape=jax.ShapeDtypeStruct((Y, 2 * ROWS +...  2.11 us
  transfers between devices with their start and end apart: 4, of which 2 were waited for; matrix products, arithmetic and copies ran while one was open for 0% of the time, Pallas kernels for 6%

commit v1 on v0

--- a/solution.py
+++ b/solution.py
@@ -22,6 +22,7 @@
 TILES = Y // 2
 GROUP = Y * SPAN
 STATS = 16
+PLACE = 3
 NEG = -1e30
 LOG2E = math.log2(math.e)
 C = LOG2E / math.sqrt(HEAD_DIM)
@@ -46,27 +47,26 @@
 
 
 def combine_kernel(in_ref, out_ref):
-    logs = []
     for h in range(HEADS):
+        logs = []
         for n in range(2):
             terms = in_ref[h, n, ROWS:, :].astype(jnp.float32)
             logs.append(terms[0:1] + terms[1:2] + terms[2:3])
-    a = jnp.concatenate(logs[::2] + logs[:1] * (8 - HEADS), axis=0)
-    b = jnp.concatenate(logs[1::2] + logs[1:2] * (8 - HEADS), axis=0)
-    top = jnp.maximum(a, b)
-    a, b = jnp.exp2(a - top), jnp.exp2(b - top)
-    total = a + b
-    shares = jnp.concatenate([a / total, b / total], axis=0).T
-    for h in range(HEADS):
-        a = in_ref[h, 0, :ROWS, :].astype(jnp.float32) * shares[:, h : h + 1]
-        b = in_ref[h, 1, :ROWS, :].astype(jnp.float32) * shares[:, 8 + h : 9 + h]
-        out_ref[:, h * HEAD_DIM : (h + 1) * HEAD_DIM] = (a + b).astype(jnp.bfloat16)
+        top = jnp.maximum(logs[0], logs[1])
+        a, b = jnp.exp2(logs[0] - top), jnp.exp2(logs[1] - top)
+        o = in_ref[h, 0, :ROWS, :].astype(jnp.float32) * (a / (a + b))
+        o += in_ref[h, 1, :ROWS, :].astype(jnp.float32) * (b / (a + b))
+        out_ref[:, h * HEAD_DIM : (h + 1) * HEAD_DIM] = o.T.astype(jnp.bfloat16)
 
 
 def combine(parts):
+    shape = (HEADS, 2, ROWS + STATS, HEAD_DIM)
     return pl.pallas_call(
         combine_kernel,
+        grid=(1,),
         out_shape=jax.ShapeDtypeStruct((ROWS, HEADS * HEAD_DIM), jnp.bfloat16),
+        in_specs=[pl.BlockSpec(shape, lambda i: (0, 0, 0, 0))],
+        out_specs=pl.BlockSpec((ROWS, HEADS * HEAD_DIM), lambda i: (0, 0)),
         name="combine",
     )(parts)
 
@@ -80,7 +80,7 @@
     )
 
 
-def find_documents(blk, x, len_ref, first_ref, lo_ref, hi_ref):
+def find_documents(blk, x, int_ref, first_ref, lo_ref, hi_ref):
     base = blk * GROUP
     pos = places(x, (8, TILE)) + lax.broadcasted_iota(jnp.int32, (8, TILE), 0) * WIDE
     lowest = jnp.minimum(x, x ^ 1) * ROWS
@@ -90,7 +90,7 @@
     los = [start] * TILES
     his = [start] * TILES
     for j in range(DOCS - 1):
-        start = start + len_ref[j]
+        start = start + int_ref[PLACE + j]
         first = jnp.where(pos >= start, start, first)
         los = [jnp.where(lowest + i * WIDE >= start, start, los[i]) for i in range(TILES)]
         his = [jnp.where(highest + i * WIDE >= start, start, his[i]) for i in range(TILES)]
@@ -100,14 +100,6 @@
         hi_ref[i] = lax.shift_right_arithmetic(his[i], WIDE_SHIFT)
 
 
-def load_block(own_ref, pair_ref, k_ref, vt_ref, j):
-    for n, ref in enumerate((own_ref, pair_ref, own_ref, pair_ref)):
-        y = 2 * j + n // 2
-        part = slice(n * ROWS, (n + 1) * ROWS)
-        k_ref[j, part, :] = ref[y, :ROWS, :]
-        vt_ref[j, :, part] = ref[y, ROWS:, :]
-
-
 def key_places(x):
     row = lax.broadcasted_iota(jnp.int32, (HALF, TILE), 0)
     return jnp.where(row < ROWS, x, X - 1 - x) * ROWS + (row & (ROWS - 1))
@@ -120,28 +112,28 @@
     )
 
 
-def scores_of(k_ref, s_ref, q, g, n, m, kept):
+def scores_of(refs, s_ref, q, g, n, m, kept):
     part = slice(n * HALF, (n + 1) * HALF)
-    s = jnp.dot(k_ref[g, part, :], q, preferred_element_type=jnp.float32)
+    k = jnp.concatenate([ref[2 * g + n, :ROWS, :] for ref in refs], axis=0)
+    s = jnp.dot(k, q, preferred_element_type=jnp.float32)
     if kept is not None:
         s = jnp.where(kept, s, NEG)
     s_ref[g, part, :] = s
     return jnp.maximum(m, jnp.max(s.reshape(HALF // 8, 8, TILE), axis=0))
 
 
-def mix(vt_ref, s_ref, g, n, shift, l, acc):
+def mix(refs, s_ref, g, n, shift, l, acc):
     part = slice(n * HALF, (n + 1) * HALF)
     p = jnp.exp2(s_ref[g, part, :] * C - shift)
     l = l + jnp.sum(p.reshape(HALF // 8, 8, TILE), axis=0)
-    acc = acc + jnp.dot(
-        vt_ref[g, :, part], p.astype(jnp.bfloat16), preferred_element_type=jnp.float32
-    )
+    vt = jnp.concatenate([ref[2 * g + n, ROWS:, :] for ref in refs], axis=1)
+    acc = acc + jnp.dot(vt, p.astype(jnp.bfloat16), preferred_element_type=jnp.float32)
     return l, acc
 
 
-def mix_block(vt_ref, s_ref, g, shift, l, acc):
+def mix_block(refs, s_ref, g, shift, l, acc):
     for n in range(2):
-        l, acc = mix(vt_ref, s_ref, g, n, shift, l, acc)
+        l, acc = mix(refs, s_ref, g, n, shift, l, acc)
     return l, acc
 
 
@@ -150,8 +142,7 @@
 
 
 def own_kernel(
-    place_ref,
-    len_ref,
+    int_ref,
     q_own_ref,
     q_pair_ref,
     own_ref,
@@ -161,22 +152,16 @@
     first_ref,
     lo_ref,
     hi_ref,
-    k_ref,
-    vt_ref,
     even_ref,
     odd_ref,
 ):
-    blk, x, slot = place_ref[0], place_ref[1], place_ref[2]
+    blk, x, slot = int_ref[0], int_ref[1], int_ref[2]
 
     @pl.when(slot < HEADS)
     def _():
-        find_documents(blk, x, len_ref, first_ref, lo_ref, hi_ref)
-
-        def load(j, _):
-            load_block(own_ref, pair_ref, k_ref, vt_ref, j)
-            return 0
-
-        lax.fori_loop(0, TILES, load, 0)
+        find_documents(blk, x, int_ref, first_ref, lo_ref, hi_ref)
+
+        refs = (own_ref, pair_ref)
         key_rows = key_places(x)
 
         def score(s_ref, i, q, g, n, m, masked, diagonal):
@@ -185,7 +170,7 @@
                 kept = key_rows >= first_ref[i : i + 1, :] - (g * WIDE + n * SPAN)
                 if diagonal:
                     kept &= key_rows <= places(x, (1, TILE)) - n * SPAN
-            return scores_of(k_ref, s_ref, q, g, n, m, kept)
+            return scores_of(refs, s_ref, q, g, n, m, kept)
 
         def score_diagonal(s_ref, i, q, m):
             for n in range(2):
@@ -209,7 +194,7 @@
                 def step(masked, g, carry, i=i, q=q, shift=shift, s_ref=s_ref, later_ref=later_ref):
                     m, l, acc = carry
                     for n in range(2):
-                        l, acc = mix(vt_ref, s_ref, g, n, shift, l, acc)
+                        l, acc = mix(refs, s_ref, g, n, shift, l, acc)
                         m = score(later_ref, i + 1, q, g, n, m, masked, False)
                     return m, l, acc
 
@@ -224,7 +209,7 @@
                 l, acc = lax.fori_loop(
                     begin,
                     i + 1,
-                    lambda g, c, s_ref=s_ref, shift=shift: mix_block(vt_ref, s_ref, g, shift, *c),
+                    lambda g, c, s_ref=s_ref, shift=shift: mix_block(refs, s_ref, g, shift, *c),
                     sums,
                 )
             l = jnp.sum(l, axis=0, keepdims=True)
@@ -234,8 +219,7 @@
 
 
 def prev_kernel(
-    place_ref,
-    len_ref,
+    int_ref,
     q_own_ref,
     q_pair_ref,
     prev_own_ref,
@@ -246,32 +230,26 @@
     first_ref,
     lo_ref,
     hi_ref,
-    k_ref,
-    vt_ref,
     even_ref,
     odd_ref,
 ):
-    blk, x, slot = place_ref[0], place_ref[1], place_ref[2]
+    blk, x, slot = int_ref[0], int_ref[1], int_ref[2]
 
     @pl.when(slot < HEADS)
     def _():
-        find_documents(blk, x, len_ref, first_ref, lo_ref, hi_ref)
+        find_documents(blk, x, int_ref, first_ref, lo_ref, hi_ref)
 
         def begin_of(i):
             return jnp.where(blk > 0, jnp.clip(lo_ref[i] + TILES, 0, TILES), TILES)
 
-        def load(j, _):
-            load_block(prev_own_ref, prev_pair_ref, k_ref, vt_ref, j)
-            return 0
-
-        lax.fori_loop(begin_of(0), TILES, load, 0)
+        refs = (prev_own_ref, prev_pair_ref)
         key_rows = key_places(x)
 
         def score(s_ref, i, q, g, n, m, masked):
             kept = None
             if masked:
                 kept = key_rows >= first_ref[i : i + 1, :] - ((g - TILES) * WIDE + n * SPAN)
-            return scores_of(k_ref, s_ref, q, g, n, m, kept)
+            return scores_of(refs, s_ref, q, g, n, m, kept)
 
         def score_first(masked, g, m):
             for n in range(2):
@@ -303,7 +281,7 @@
                 def step(masked, g, carry, i=i, q=q, shift=shift, s_ref=s_ref, later_ref=later_ref):
                     m, l, acc = carry
                     for n in range(2):
-                        l, acc = mix(vt_ref, s_ref, g, n, shift, l, acc)
+                        l, acc = mix(refs, s_ref, g, n, shift, l, acc)
                         m = score(later_ref, i + 1, q, g, n, m, masked)
                     return m, l, acc
 
@@ -315,13 +293,13 @@
                 l, acc = lax.fori_loop(
                     begin,
                     TILES,
-                    lambda g, c, s_ref=s_ref, shift=shift: mix_block(vt_ref, s_ref, g, shift, *c),
+                    lambda g, c, s_ref=s_ref, shift=shift: mix_block(refs, s_ref, g, shift, *c),
                     sums,
                 )
             l = jnp.sum(l, axis=0, keepdims=True) + own_l * scale
             some = l > 0.0
             l = jnp.where(some, l, 1.0)
-            o = acc / l
+            o = (acc * (1.0 / l)).astype(jnp.bfloat16)
             log = jnp.where(some, shift + jnp.log(l) * LOG2E, NEG)
             high = log.astype(jnp.bfloat16).astype(jnp.float32)
             middle = (log - high).astype(jnp.bfloat16).astype(jnp.float32)
@@ -332,7 +310,7 @@
             for n in range(4):
                 part = slice(n * ROWS, (n + 1) * ROWS)
                 y, to = 2 * i + (n & 1), (x & 1) ^ (n >> 1)
-                o_ref[y, to, :ROWS, :] = o[:, part].T.astype(jnp.bfloat16)
+                o_ref[y, to, :ROWS, :] = o[:, part]
                 o_ref[y, to, ROWS:, :] = stats[:, part]
 
 
@@ -340,8 +318,6 @@
     pltpu.VMEM((8, TILE), jnp.int32),
     pltpu.SMEM((TILES,), jnp.int32),
     pltpu.SMEM((TILES,), jnp.int32),
-    pltpu.VMEM((TILES, TILE, HEAD_DIM), jnp.bfloat16),
-    pltpu.VMEM((TILES, HEAD_DIM, TILE), jnp.bfloat16),
     pltpu.VMEM((TILES, TILE, TILE), jnp.float32),
     pltpu.VMEM((TILES, TILE, TILE), jnp.float32),
 ]
@@ -350,51 +326,52 @@
 ACC = (TILES, HEAD_DIM, TILE)
 
 
-def attend_own(place, lengths, q_own, q_pair, own, pair):
+def attend_own(ints, q_own, q_pair, own, pair):
     return pl.pallas_call(
         own_kernel,
         out_shape=(
             jax.ShapeDtypeStruct(ACC, jnp.float32),
             jax.ShapeDtypeStruct((TILES, 8, TILE), jnp.float32),
         ),
-        in_specs=[SMEM, SMEM] + [VMEM] * 4,
+        in_specs=[SMEM] + [VMEM] * 4,
         out_specs=(VMEM, VMEM),
         scratch_shapes=SCRATCH,
-        compiler_params=pltpu.CompilerParams(vmem_limit_bytes=20 << 20),
+        compiler_params=pltpu.CompilerParams(vmem_limit_bytes=16 << 20),
         cost_estimate=pl.CostEstimate(
             flops=1 << 30, bytes_accessed=4 << 20, transcendentals=2 << 20
         ),
         name="attend_own",
-    )(place, lengths, q_own, q_pair, own, pair)
-
-
-def attend_prev(place, lengths, q_own, q_pair, prev_own, prev_pair, acc, state):
+    )(ints, q_own, q_pair, own, pair)
+
+
+def attend_prev(ints, q_own, q_pair, prev_own, prev_pair, acc, state):
     return pl.pallas_call(
         prev_kernel,
         out_shape=jax.ShapeDtypeStruct((Y, 2, ROWS + STATS, HEAD_DIM), jnp.bfloat16),
-        in_specs=[SMEM, SMEM] + [VMEM] * 6,
+        in_specs=[SMEM] + [VMEM] * 6,
         out_specs=VMEM,
         scratch_shapes=SCRATCH,
-        compiler_params=pltpu.CompilerParams(vmem_limit_bytes=20 << 20),
+        compiler_params=pltpu.CompilerParams(vmem_limit_bytes=16 << 20),
         cost_estimate=pl.CostEstimate(
             flops=1 << 29, bytes_accessed=4 << 20, transcendentals=1 << 20
         ),
         name="attend_prev",
-    )(place, lengths, q_own, q_pair, prev_own, prev_pair, acc, state)
+    )(ints, q_own, q_pair, prev_own, prev_pair, acc, state)
 
 
 def body(queries, keys, values, lengths):
     x = 2 * lax.axis_index("xh") + lax.axis_index("xl")
     place = jnp.stack([lax.axis_index("blk"), x, lax.axis_index("y")]).astype(jnp.int32)
+    ints = jnp.concatenate([place, lengths])
     got = lax.all_to_all(pack(queries, keys, values), "y", 0, 0, tiled=True)
     own_queries, own = got[:, :ROWS], got[:, ROWS:]
     pair = lax.ppermute(own, ("xh", "xl"), KEY_PAIRS)
     pair_queries = lax.ppermute(own_queries, "xl", QUERY_PAIRS)
     prev_own = lax.ppermute(own, "blk", [(0, 1)])
-    pair, pair_queries = lax.optimization_barrier((pair, pair_queries))
+    pair, pair_queries, ints = lax.optimization_barrier((pair, pair_queries, ints))
     prev_pair = lax.ppermute(pair, "blk", [(0, 1)])
-    state = attend_own(place, lengths, own_queries, pair_queries, own, pair)
-    parts = attend_prev(place, lengths, own_queries, pair_queries, prev_own, prev_pair, *state)
+    state = attend_own(ints, own_queries, pair_queries, own, pair)
+    parts = attend_prev(ints, own_queries, pair_queries, prev_own, prev_pair, *state)
     parts = parts.reshape(2 * Y, ROWS + STATS, HEAD_DIM)
     parts = lax.all_to_all(parts, ("y", "xl"), 0, 0, tiled=True)
     return combine(parts.reshape(Y, 2, ROWS + STATS, HEAD_DIM))

time: 83.6 us -> 81.9 us (0.980)
  Pallas kernels: 16.2 us -> 15.2 us
where the time goes in v1:
time: 81.9 us; the launch traced here: 81.6 us
  blocking collectives  49.7 us (61%)
  Pallas kernels  15.2 us (19%)
  starting transfers between devices  10.5 us (13%)
  waiting for transfers between devices  5.31 us (6%)
    all_to_all x1, blocking collectives, body(): got = lax.all_to_all(pack(queries, keys, values), 'y', 0, 0, tiled=True)  27.6 us
    all_to_all x1, blocking collectives, body(): parts = lax.all_to_all(parts, ('y', 'xl'), 0, 0, tiled=True)  22.1 us
    pallas_call x1, Pallas kernels, attend_prev(): pl.pallas_call(prev_kernel, out_shape=jax.ShapeDtypeStruct((Y, 2, ROWS +...  6.25 us
    ppermute x1, starting transfers between devices, body(): pair = lax.ppermute(own, ('xh', 'xl'), KEY_PAIRS)  6.03 us
    pallas_call x1, Pallas kernels, attend_own(): pl.pallas_call(own_kernel, out_shape=(jax.ShapeDtypeStruct(ACC, jnp.float...  5.02 us
    ppermute x1, waiting for transfers between devices, body(): pair_queries = lax.ppermute(own_queries, 'xl', QUERY_PAIRS)  3.45 us
    pallas_call x1, Pallas kernels, pack(): pl.pallas_call(pack_kernel, out_shape=jax.ShapeDtypeStruct((Y, 2 * ROWS +...  2.11 us
    ppermute x1, starting transfers between devices, body(): pair_queries = lax.ppermute(own_queries, 'xl', QUERY_PAIRS)  1.92 us
  transfers between devices with their start and end apart: 4, of which 2 were waited for; matrix products, arithmetic and copies ran while one was open for 0% of the time, Pallas kernels for 6%

profile of v1, /device:TPU:1, one launch (start us, length us, event | category | flops | bytes accessed | tf_op | source)
XLA Modules:
  0.0 81.6 jit_solution(1618310522744743371)
XLA Ops:
  0.0 2.1 %pack.1 = bf16[8,384,128]{2,1,0:T(8,128)(2,1)} custom-call(bf16[128,640]{1,0:T(8,128)(2,1)} %q_ref.1, bf16[128,640]{1,0:T(8,128)(2,1)} %k_ref.1, bf16[128,640]{1,0:T(8,128)(2,1)} %v_ref.1), custom_call_target="tpu_custom_call" | custom-call | tf_op jit(solution)/shard_map/pack/pallas_call | solution.py:42
  2.1 27.6 %all_to_all.10 = bf16[8,384,128]{2,1,0:T(8,128)(2,1)S(1)} all-to-all(bf16[8,384,128]{2,1,0:T(8,128)(2,1)} %pack.1), channel_id=1, replica_groups=mesh['blk'=2,'y'=8,'xh'=2,'xl'=2,'tp'=8] {'y'}, dimensions={0} | all-to-all | bytes 1572864 | tf_op jit(solution)/shard_map/all_to_all | solution.py:366
  29.8 6.0 %collective-permute-start = (bf16[8,256,128]{2,1,0:T(8,128)(2,1)S(1)}, bf16[8,256,128]{2,1,0:T(8,128)(2,1)S(1)}, u32[]{:S(2)}, u32[]{:S(2)}) collective-permute-start(bf16[8,256,128]{2,1,0:T(8,128)(2,1)S(1)} %slice.8.own_ref), channel_id=1, source_target_pairs={{0,24},{8,16},{16,8},{24,0},{1,25},{9,17},{17,9},{25,1},{2,26},{10... | collective-permute-start | bytes 1572872 | tf_op jit(solution)/shard_map/ppermute | solution.py:368
  35.8 1.9 %collective-permute-start.1 = (bf16[8,128,128]{2,1,0:T(8,128)(2,1)S(1)}, bf16[8,128,128]{2,1,0:T(8,128)(2,1)S(1)}, u32[]{:S(2)}, u32[]{:S(2)}) collective-permute-start(bf16[8,128,128]{2,1,0:T(8,128)(2,1)S(1)} %slice.9.q_own_ref), channel_id=1, source_target_pairs={{0,8},{8,0},{1,9},{9,1},{2,10},{10,2},{3,11},{11,3},{4,12},{12,4},... | collective-permute-start | bytes 786440 | tf_op jit(solution)/shard_map/ppermute | solution.py:369
  37.8 0.0 copy-start
  37.8 0.6 copy-done
  38.4 0.1 pad_add_fusion.int_ref
  38.5 1.3 %collective-permute-start.2 = (bf16[8,256,128]{2,1,0:T(8,128)(2,1)S(1)}, bf16[8,256,128]{2,1,0:T(8,128)(2,1)S(1)}, u32[]{:S(2)}, u32[]{:S(2)}) collective-permute-start(bf16[8,256,128]{2,1,0:T(8,128)(2,1)S(1)} %slice.8.own_ref), channel_id=1, source_target_pairs={{0,256},{1,257},{2,258},{3,259},{4,260},{5,261},{6,262},{7,263},{8... | collective-permute-start | bytes 1572872 | tf_op jit(solution)/shard_map/ppermute | solution.py:370
  39.8 3.4 %collective-permute-done.1.q_pair_ref = bf16[8,128,128]{2,1,0:T(8,128)(2,1)S(1)} collective-permute-done((bf16[8,128,128]{2,1,0:T(8,128)(2,1)S(1)}, bf16[8,128,128]{2,1,0:T(8,128)(2,1)S(1)}, u32[]{:S(2)}, u32[]{:S(2)}) %collective-permute-start.1) | collective-permute-done | bytes 262176 | tf_op jit(solution)/shard_map/ppermute | solution.py:369
  43.2 1.9 %collective-permute-done.pair_ref = bf16[8,256,128]{2,1,0:T(8,128)(2,1)S(1)} collective-permute-done((bf16[8,256,128]{2,1,0:T(8,128)(2,1)S(1)}, bf16[8,256,128]{2,1,0:T(8,128)(2,1)S(1)}, u32[]{:S(2)}, u32[]{:S(2)}) %collective-permute-start) | collective-permute-done | bytes 524320 | tf_op jit(solution)/shard_map/ppermute | solution.py:368
  45.1 1.3 %collective-permute-start.3 = (bf16[8,256,128]{2,1,0:T(8,128)(2,1)S(1)}, bf16[8,256,128]{2,1,0:T(8,128)(2,1)S(1)}, u32[]{:S(2)}, u32[]{:S(2)}) collective-permute-start(bf16[8,256,128]{2,1,0:T(8,128)(2,1)S(1)} %collective-permute-done.pair_ref), channel_id=1, source_target_pairs={{0,256},{1,257},{2,258},{3,259},{4,260},{5,261},{6,262},{7,263},{8... | collective-permute-start | bytes 1572872 | tf_op jit(solution)/shard_map/ppermute | solution.py:372
  46.4 5.0 %attend_own.1 = (f32[4,128,512]{2,1,0:T(8,128)S(1)}, f32[4,8,512]{2,1,0:T(8,128)S(1)}) custom-call(s32[35]{0:T(128)S(1)} %pad_add_fusion.int_ref, bf16[8,128,128]{2,1,0:T(8,128)(2,1)S(1)} %slice.9.q_own_ref, bf16[8,128,128]{2,1,0:T(8,128)(2,1)S(1)} %collective-permute-done.1.q_pair_ref, bf16[8,256,128]{2,1,0:T(8,128)(2,1)S(1)} %slice.8.own_ref, ...), custom_call_target="tpu_custom_call" | custom-call | flops 1073741824 | bytes 4194304 | tf_op jit(solution)/shard_map/attend_own/pallas_call | solution.py:330
  51.4 0.0 collective-permute-done.2.prev_own_ref
  51.4 0.0 collective-permute-done.3.prev_pair_ref
  51.4 6.3 %attend_prev.1 = bf16[8,2,144,128]{3,2,1,0:T(8,128)(2,1)S(1)} custom-call(s32[35]{0:T(128)S(1)} %pad_add_fusion.int_ref, bf16[8,128,128]{2,1,0:T(8,128)(2,1)S(1)} %slice.9.q_own_ref, bf16[8,128,128]{2,1,0:T(8,128)(2,1)S(1)} %collective-permute-done.1.q_pair_ref, bf16[8,256,128]{2,1,0:T(8,128)(2,1)S(1)} %collective-permute-done.2.prev_own_ref, ...), custom_call_target="tpu_custom_call" | custom-call | flops 536870912 | bytes 4194304 | tf_op jit(solution)/shard_map/attend_prev/pallas_call | solution.py:348
  57.7 22.1 %all_to_all.11 = bf16[16,144,128]{2,1,0:T(8,128)(2,1)} all-to-all(bf16[16,144,128]{2,1,0:T(8,128)(2,1)S(1)} %bitcast.5), channel_id=1, replica_groups=mesh['blk'=2,'y'=8,'xh'=2,'xl'=2,'tp'=8] {'y','xl'}, dimensions={0} | all-to-all | bytes 1179648 | tf_op jit(solution)/shard_map/all_to_all | solution.py:376
  79.8 1.8 %combine.1 = bf16[128,640]{1,0:T(8,128)(2,1)} custom-call(bf16[8,2,144,128]{3,2,1,0:T(8,128)(2,1)} %bitcast.6), custom_call_target="tpu_custom_call" | custom-call | tf_op jit(solution)/shard_map/combine/pallas_call | solution.py:64
  (2 shorter events, 0.1 us)
Async XLA Ops:
  29.8 15.3 %collective-permute-start = (bf16[8,256,128]{2,1,0:T(8,128)(2,1)S(1)}, bf16[8,256,128]{2,1,0:T(8,128)(2,1)S(1)}, u32[]{:S(2)}, u32[]{:S(2)}) collective-permute-start(bf16[8,256,128]{2,1,0:T(8,128)(2,1)S(1)} %slice.8.own_ref), channel_id=1, source_target_pairs={{0,24},{8,16},{16,8},{24,0},{1,25},{9,17},{17,9},{25,1},{2,26},{10... | collective-permute-start | bytes 1572872 | tf_op jit(solution)/shard_map/ppermute | solution.py:368
  35.8 7.4 %collective-permute-start.1 = (bf16[8,128,128]{2,1,0:T(8,128)(2,1)S(1)}, bf16[8,128,128]{2,1,0:T(8,128)(2,1)S(1)}, u32[]{:S(2)}, u32[]{:S(2)}) collective-permute-start(bf16[8,128,128]{2,1,0:T(8,128)(2,1)S(1)} %slice.9.q_own_ref), channel_id=1, source_target_pairs={{0,8},{8,0},{1,9},{9,1},{2,10},{10,2},{3,11},{11,3},{4,12},{12,4},... | collective-permute-start | bytes 786440 | tf_op jit(solution)/shard_map/ppermute | solution.py:369
  37.8 0.7 copy-start
  38.5 12.9 %collective-permute-start.2 = (bf16[8,256,128]{2,1,0:T(8,128)(2,1)S(1)}, bf16[8,256,128]{2,1,0:T(8,128)(2,1)S(1)}, u32[]{:S(2)}, u32[]{:S(2)}) collective-permute-start(bf16[8,256,128]{2,1,0:T(8,128)(2,1)S(1)} %slice.8.own_ref), channel_id=1, source_target_pairs={{0,256},{1,257},{2,258},{3,259},{4,260},{5,261},{6,262},{7,263},{8... | collective-permute-start | bytes 1572872 | tf_op jit(solution)/shard_map/ppermute | solution.py:370
  45.1 6.3 %collective-permute-start.3 = (bf16[8,256,128]{2,1,0:T(8,128)(2,1)S(1)}, bf16[8,256,128]{2,1,0:T(8,128)(2,1)S(1)}, u32[]{:S(2)}, u32[]{:S(2)}) collective-permute-start(bf16[8,256,128]{2,1,0:T(8,128)(2,1)S(1)} %collective-permute-done.pair_ref), channel_id=1, source_target_pairs={{0,256},{1,257},{2,258},{3,259},{4,260},{5,261},{6,262},{7,263},{8... | collective-permute-start | bytes 1572872 | tf_op jit(solution)/shard_map/ppermute | solution.py:372

commit v2 on v1

--- a/solution.py
+++ b/solution.py
@@ -30,6 +30,10 @@
 QUERY_PAIRS = [(0, 1), (1, 0)]
 
 
+SMEM = pl.BlockSpec(memory_space=pltpu.SMEM)
+VMEM = pl.BlockSpec(memory_space=pltpu.VMEM)
+
+
 def pack_kernel(q_ref, k_ref, v_ref, out_ref):
     for h in range(HEADS):
         cols = slice(h * HEAD_DIM, (h + 1) * HEAD_DIM)
@@ -46,29 +50,46 @@
     )(q, k, v)
 
 
-def combine_kernel(in_ref, out_ref):
+def merge_kernel(int_ref, mine_ref, theirs_ref, out_ref):
+    @pl.when(int_ref[2] < HEADS)
+    def _():
+        for y in range(Y):
+            logs = []
+            for ref in (mine_ref, theirs_ref):
+                terms = ref[y, ROWS:, :].astype(jnp.float32)
+                logs.append(terms[0:1] + terms[1:2] + terms[2:3])
+            top = jnp.maximum(logs[0], logs[1])
+            a, b = jnp.exp2(logs[0] - top), jnp.exp2(logs[1] - top)
+            o = mine_ref[y, :ROWS, :].astype(jnp.float32) * (a / (a + b))
+            o += theirs_ref[y, :ROWS, :].astype(jnp.float32) * (b / (a + b))
+            out_ref[y] = o.astype(jnp.bfloat16)
+
+
+def merge(ints, mine, theirs):
+    return pl.pallas_call(
+        merge_kernel,
+        out_shape=jax.ShapeDtypeStruct((Y, HEAD_DIM, ROWS), jnp.bfloat16),
+        in_specs=[SMEM, VMEM, VMEM],
+        out_specs=VMEM,
+        name="merge",
+    )(ints, mine, theirs)
+
+
+def unpack_kernel(in_ref, out_ref):
     for h in range(HEADS):
-        logs = []
-        for n in range(2):
-            terms = in_ref[h, n, ROWS:, :].astype(jnp.float32)
-            logs.append(terms[0:1] + terms[1:2] + terms[2:3])
-        top = jnp.maximum(logs[0], logs[1])
-        a, b = jnp.exp2(logs[0] - top), jnp.exp2(logs[1] - top)
-        o = in_ref[h, 0, :ROWS, :].astype(jnp.float32) * (a / (a + b))
-        o += in_ref[h, 1, :ROWS, :].astype(jnp.float32) * (b / (a + b))
-        out_ref[:, h * HEAD_DIM : (h + 1) * HEAD_DIM] = o.T.astype(jnp.bfloat16)
-
-
-def combine(parts):
-    shape = (HEADS, 2, ROWS + STATS, HEAD_DIM)
+        out_ref[:, h * HEAD_DIM : (h + 1) * HEAD_DIM] = in_ref[h].T
+
+
+def unpack(o):
+    shape = (HEADS, HEAD_DIM, ROWS)
     return pl.pallas_call(
-        combine_kernel,
+        unpack_kernel,
         grid=(1,),
         out_shape=jax.ShapeDtypeStruct((ROWS, HEADS * HEAD_DIM), jnp.bfloat16),
-        in_specs=[pl.BlockSpec(shape, lambda i: (0, 0, 0, 0))],
+        in_specs=[pl.BlockSpec(shape, lambda i: (0, 0, 0))],
         out_specs=pl.BlockSpec((ROWS, HEADS * HEAD_DIM), lambda i: (0, 0)),
-        name="combine",
-    )(parts)
+        name="unpack",
+    )(o)
 
 
 def places(x, shape):
@@ -226,7 +247,8 @@
     prev_pair_ref,
     acc_ref,
     state_ref,
-    o_ref,
+    mine_ref,
+    theirs_ref,
     first_ref,
     lo_ref,
     hi_ref,
@@ -309,9 +331,9 @@
             stats = stats.astype(jnp.bfloat16)
             for n in range(4):
                 part = slice(n * ROWS, (n + 1) * ROWS)
-                y, to = 2 * i + (n & 1), (x & 1) ^ (n >> 1)
-                o_ref[y, to, :ROWS, :] = o[:, part]
-                o_ref[y, to, ROWS:, :] = stats[:, part]
+                ref = mine_ref if n < 2 else theirs_ref
+                ref[2 * i + (n & 1), :ROWS, :] = o[:, part]
+                ref[2 * i + (n & 1), ROWS:, :] = stats[:, part]
 
 
 SCRATCH = [
@@ -321,8 +343,6 @@
     pltpu.VMEM((TILES, TILE, TILE), jnp.float32),
     pltpu.VMEM((TILES, TILE, TILE), jnp.float32),
 ]
-SMEM = pl.BlockSpec(memory_space=pltpu.SMEM)
-VMEM = pl.BlockSpec(memory_space=pltpu.VMEM)
 ACC = (TILES, HEAD_DIM, TILE)
 
 
@@ -347,9 +367,9 @@
 def attend_prev(ints, q_own, q_pair, prev_own, prev_pair, acc, state):
     return pl.pallas_call(
         prev_kernel,
-        out_shape=jax.ShapeDtypeStruct((Y, 2, ROWS + STATS, HEAD_DIM), jnp.bfloat16),
+        out_shape=(jax.ShapeDtypeStruct((Y, HEAD_DIM + STATS, ROWS), jnp.bfloat16),) * 2,
         in_specs=[SMEM] + [VMEM] * 6,
-        out_specs=VMEM,
+        out_specs=(VMEM, VMEM),
         scratch_shapes=SCRATCH,
         compiler_params=pltpu.CompilerParams(vmem_limit_bytes=16 << 20),
         cost_estimate=pl.CostEstimate(
@@ -371,10 +391,10 @@
     pair, pair_queries, ints = lax.optimization_barrier((pair, pair_queries, ints))
     prev_pair = lax.ppermute(pair, "blk", [(0, 1)])
     state = attend_own(ints, own_queries, pair_queries, own, pair)
-    parts = attend_prev(ints, own_queries, pair_queries, prev_own, prev_pair, *state)
-    parts = parts.reshape(2 * Y, ROWS + STATS, HEAD_DIM)
-    parts = lax.all_to_all(parts, ("y", "xl"), 0, 0, tiled=True)
-    return combine(parts.reshape(Y, 2, ROWS + STATS, HEAD_DIM))
+    mine, theirs = attend_prev(ints, own_queries, pair_queries, prev_own, prev_pair, *state)
+    theirs = lax.ppermute(theirs, "xl", QUERY_PAIRS)
+    o = merge(ints, mine, theirs)
+    return unpack(lax.all_to_all(o, "y", 0, 0, tiled=True))
 
 
 def solution(mesh):

time: 81.9 us -> 88.7 us (1.083)
  waiting for transfers between devices: 5.31 us -> 12.4 us
  blocking collectives: 49.7 us -> 44 us
  starting transfers between devices: 10.5 us -> 12.8 us
  Pallas kernels: 15.2 us -> 16.7 us
  local copies, waits for them, and re-layouts: 0.7 us -> 2.13 us
    ppermute x0 -> x1, waiting for transfers between devices: none -> 7.11 us  [body(): theirs = lax.ppermute(theirs, 'xl', QUERY_PAIRS)]
    all_to_all x1, blocking collectives: 22.1 us -> 16.4 us  [body(): return unpack(lax.all_to_all(o, 'y', 0, 0, tiled=True))]
    ppermute x0 -> x1, starting transfers between devices: none -> 2.27 us  [body(): theirs = lax.ppermute(theirs, 'xl', QUERY_PAIRS)]
    unnamed x2 -> x8, local copies, waits for them, and re-layouts: 0.65 us -> 2.08 us
    pallas_call x2 -> x3, Pallas kernels: 8.07 us -> 8.94 us  [the longest x1 5.33 us: attend_prev(): pl.pallas_call(prev_kernel, out_shape=(jax.ShapeDtypeStruct((Y, HEAD_DIM...]
  transfers between devices with their start and end apart: 4 -> 5, of which waited for: 2 -> 3; matrix products, arithmetic and copies ran while one was open for 0% -> 0% of each run, Pallas kernels for 6% -> 6%
where the time goes in v2:
time: 88.7 us; the launch traced here: 88.3 us
  blocking collectives  44 us (50%)
  Pallas kernels  16.7 us (19%)
  starting transfers between devices  12.8 us (14%)
  waiting for transfers between devices  12.4 us (14%)
  local copies, waits for them, and re-layouts  2.13 us (2%)
    all_to_all x1, blocking collectives, body(): got = lax.all_to_all(pack(queries, keys, values), 'y', 0, 0, tiled=True)  27.6 us
    all_to_all x1, blocking collectives, body(): return unpack(lax.all_to_all(o, 'y', 0, 0, tiled=True))  16.4 us
    ppermute x1, waiting for transfers between devices, body(): theirs = lax.ppermute(theirs, 'xl', QUERY_PAIRS)  7.11 us
    ppermute x1, starting transfers between devices, body(): pair = lax.ppermute(own, ('xh', 'xl'), KEY_PAIRS)  6.03 us
    pallas_call x1, Pallas kernels, attend_own(): pl.pallas_call(own_kernel, out_shape=(jax.ShapeDtypeStruct(ACC, jnp.float...  5.72 us
    pallas_call x1, Pallas kernels, attend_prev(): pl.pallas_call(prev_kernel, out_shape=(jax.ShapeDtypeStruct((Y, HEAD_DIM...  5.33 us
    ppermute x1, waiting for transfers between devices, body(): pair_queries = lax.ppermute(own_queries, 'xl', QUERY_PAIRS)  3.45 us
    ppermute x1, starting transfers between devices, body(): theirs = lax.ppermute(theirs, 'xl', QUERY_PAIRS)  2.27 us
  transfers between devices with their start and end apart: 5, of which 3 were waited for; matrix products, arithmetic and copies ran while one was open for 0% of the time, Pallas kernels for 6%

profile of v2, /device:TPU:1, one launch (start us, length us, event | category | flops | bytes accessed | tf_op | source)
XLA Modules:
  0.0 88.3 jit_solution(8011660074163889045)
XLA Ops:
  0.0 2.1 %pack.1 = bf16[8,384,128]{2,1,0:T(8,128)(2,1)} custom-call(bf16[128,640]{1,0:T(8,128)(2,1)} %q_ref.1, bf16[128,640]{1,0:T(8,128)(2,1)} %k_ref.1, bf16[128,640]{1,0:T(8,128)(2,1)} %v_ref.1), custom_call_target="tpu_custom_call" | custom-call | tf_op jit(solution)/shard_map/pack/pallas_call | solution.py:46
  2.1 27.6 %all_to_all.10 = bf16[8,384,128]{2,1,0:T(8,128)(2,1)S(1)} all-to-all(bf16[8,384,128]{2,1,0:T(8,128)(2,1)} %pack.1), channel_id=1, replica_groups=mesh['blk'=2,'y'=8,'xh'=2,'xl'=2,'tp'=8] {'y'}, dimensions={0} | all-to-all | bytes 1572864 | tf_op jit(solution)/shard_map/all_to_all | solution.py:386
  29.7 6.0 %collective-permute-start = (bf16[8,256,128]{2,1,0:T(8,128)(2,1)S(1)}, bf16[8,256,128]{2,1,0:T(8,128)(2,1)S(1)}, u32[]{:S(2)}, u32[]{:S(2)}) collective-permute-start(bf16[8,256,128]{2,1,0:T(8,128)(2,1)S(1)} %slice.8.own_ref), channel_id=1, source_target_pairs={{0,24},{8,16},{16,8},{24,0},{1,25},{9,17},{17,9},{25,1},{2,26},{10... | collective-permute-start | bytes 1572872 | tf_op jit(solution)/shard_map/ppermute | solution.py:388
  35.8 1.9 %collective-permute-start.1 = (bf16[8,128,128]{2,1,0:T(8,128)(2,1)S(1)}, bf16[8,128,128]{2,1,0:T(8,128)(2,1)S(1)}, u32[]{:S(2)}, u32[]{:S(2)}) collective-permute-start(bf16[8,128,128]{2,1,0:T(8,128)(2,1)S(1)} %slice.9.q_own_ref), channel_id=1, source_target_pairs={{0,8},{8,0},{1,9},{9,1},{2,10},{10,2},{3,11},{11,3},{4,12},{12,4},... | collective-permute-start | bytes 786440 | tf_op jit(solution)/shard_map/ppermute | solution.py:389
  37.7 0.0 copy-start.3
  37.8 0.6 copy-done.3
  38.4 0.1 pad_add_fusion.int_ref
  38.5 0.0 copy-start.1
  38.5 1.3 %collective-permute-start.2 = (bf16[8,256,128]{2,1,0:T(8,128)(2,1)S(1)}, bf16[8,256,128]{2,1,0:T(8,128)(2,1)S(1)}, u32[]{:S(2)}, u32[]{:S(2)}) collective-permute-start(bf16[8,256,128]{2,1,0:T(8,128)(2,1)S(1)} %slice.8.own_ref), channel_id=1, source_target_pairs={{0,256},{1,257},{2,258},{3,259},{4,260},{5,261},{6,262},{7,263},{8... | collective-permute-start | bytes 1572872 | tf_op jit(solution)/shard_map/ppermute | solution.py:390
  39.8 3.4 %collective-permute-done.1.q_pair_ref = bf16[8,128,128]{2,1,0:T(8,128)(2,1)S(1)} collective-permute-done((bf16[8,128,128]{2,1,0:T(8,128)(2,1)S(1)}, bf16[8,128,128]{2,1,0:T(8,128)(2,1)S(1)}, u32[]{:S(2)}, u32[]{:S(2)}) %collective-permute-start.1) | collective-permute-done | bytes 262176 | tf_op jit(solution)/shard_map/ppermute | solution.py:389
  43.2 1.9 %collective-permute-done.pair_ref = bf16[8,256,128]{2,1,0:T(8,128)(2,1)S(1)} collective-permute-done((bf16[8,256,128]{2,1,0:T(8,128)(2,1)S(1)}, bf16[8,256,128]{2,1,0:T(8,128)(2,1)S(1)}, u32[]{:S(2)}, u32[]{:S(2)}) %collective-permute-start) | collective-permute-done | bytes 524320 | tf_op jit(solution)/shard_map/ppermute | solution.py:388
  45.1 1.3 %collective-permute-start.3 = (bf16[8,256,128]{2,1,0:T(8,128)(2,1)S(1)}, bf16[8,256,128]{2,1,0:T(8,128)(2,1)S(1)}, u32[]{:S(2)}, u32[]{:S(2)}) collective-permute-start(bf16[8,256,128]{2,1,0:T(8,128)(2,1)S(1)} %collective-permute-done.pair_ref), channel_id=1, source_target_pairs={{0,256},{1,257},{2,258},{3,259},{4,260},{5,261},{6,262},{7,263},{8... | collective-permute-start | bytes 1572872 | tf_op jit(solution)/shard_map/ppermute | solution.py:392
  46.4 5.7 %attend_own.1 = (f32[4,128,512]{2,1,0:T(8,128)S(1)}, f32[4,8,512]{2,1,0:T(8,128)S(1)}) custom-call(s32[35]{0:T(128)S(1)} %pad_add_fusion.int_ref, bf16[8,128,128]{2,1,0:T(8,128)(2,1)S(1)} %slice.9.q_own_ref, bf16[8,128,128]{2,1,0:T(8,128)(2,1)S(1)} %collective-permute-done.1.q_pair_ref, bf16[8,256,128]{2,1,0:T(8,128)(2,1)S(1)} %slice.8.own_ref, ...), custom_call_target="tpu_custom_call" | custom-call | flops 1073741824 | bytes 4194304 | tf_op jit(solution)/shard_map/attend_own/pallas_call | solution.py:350
  52.1 0.0 collective-permute-done.2.prev_own_ref
  52.1 0.0 collective-permute-done.3.prev_pair_ref
  52.1 0.0 copy-done.1
  52.1 5.3 %attend_prev.1 = (bf16[8,144,128]{2,1,0:T(8,128)(2,1)S(1)}, bf16[8,144,128]{2,1,0:T(8,128)(2,1)S(1)}) custom-call(s32[35]{0:T(128)S(1)} %pad_add_fusion.int_ref, bf16[8,128,128]{2,1,0:T(8,128)(2,1)S(1)} %slice.9.q_own_ref, bf16[8,128,128]{2,1,0:T(8,128)(2,1)S(1)} %collective-permute-done.1.q_pair_ref, ...), custom_call_target="tpu_custom_call" | custom-call | flops 536870912 | bytes 4194304 | tf_op jit(solution)/shard_map/attend_prev/pallas_call | solution.py:368
  57.5 0.0 copy-start
  57.5 0.7 copy-done
  58.2 2.3 %collective-permute-start.4 = (bf16[8,144,128]{2,1,0:T(8,128)(2,1)S(1)}, bf16[8,144,128]{2,1,0:T(8,128)(2,1)S(1)}, u32[]{:S(2)}, u32[]{:S(2)}) collective-permute-start(bf16[8,144,128]{2,1,0:T(8,128)(2,1)S(1)} %get-tuple-element.18), channel_id=1, source_target_pairs={{0,8},{8,0},{1,9},{9,1},{2,10},{10,2},{3,11},{11,3},{4,12},{12,4},... | collective-permute-start | bytes 884744 | tf_op jit(solution)/shard_map/ppermute | solution.py:395
  60.5 7.1 %collective-permute-done.4.theirs_ref = bf16[8,144,128]{2,1,0:T(8,128)(2,1)S(1)} collective-permute-done((bf16[8,144,128]{2,1,0:T(8,128)(2,1)S(1)}, bf16[8,144,128]{2,1,0:T(8,128)(2,1)S(1)}, u32[]{:S(2)}, u32[]{:S(2)}) %collective-permute-start.4) | collective-permute-done | bytes 294944 | tf_op jit(solution)/shard_map/ppermute | solution.py:395
  67.6 0.0 copy-start.2
  67.6 0.7 copy-done.2
  68.3 1.9 %merge.1 = bf16[8,128,128]{2,1,0:T(8,128)(2,1)} custom-call(s32[35]{0:T(128)} %copy-done.1, bf16[8,144,128]{2,1,0:T(8,128)(2,1)} %copy-done, bf16[8,144,128]{2,1,0:T(8,128)(2,1)} %copy-done.2), custom_call_target="tpu_custom_call" | custom-call | tf_op jit(solution)/shard_map/merge/pallas_call | solution.py:69
  70.2 16.4 %all_to_all.11.in_ref = bf16[8,128,128]{2,1,0:T(8,128)(2,1)} all-to-all(bf16[8,128,128]{2,1,0:T(8,128)(2,1)} %merge.1), channel_id=1, replica_groups=mesh['blk'=2,'y'=8,'xh'=2,'xl'=2,'tp'=8] {'y'}, dimensions={0} | all-to-all | bytes 524288 | tf_op jit(solution)/shard_map/all_to_all | solution.py:397
  86.6 1.7 %unpack.1 = bf16[128,640]{1,0:T(8,128)(2,1)} custom-call(bf16[8,128,128]{2,1,0:T(8,128)(2,1)} %all_to_all.11.in_ref), custom_call_target="tpu_custom_call" | custom-call | tf_op jit(solution)/shard_map/unpack/pallas_call | solution.py:85
  (2 shorter events, 0.1 us)
Async XLA Ops:
  29.7 15.3 %collective-permute-start = (bf16[8,256,128]{2,1,0:T(8,128)(2,1)S(1)}, bf16[8,256,128]{2,1,0:T(8,128)(2,1)S(1)}, u32[]{:S(2)}, u32[]{:S(2)}) collective-permute-start(bf16[8,256,128]{2,1,0:T(8,128)(2,1)S(1)} %slice.8.own_ref), channel_id=1, source_target_pairs={{0,24},{8,16},{16,8},{24,0},{1,25},{9,17},{17,9},{25,1},{2,26},{10... | collective-permute-start | bytes 1572872 | tf_op jit(solution)/shard_map/ppermute | solution.py:388
  35.8 7.4 %collective-permute-start.1 = (bf16[8,128,128]{2,1,0:T(8,128)(2,1)S(1)}, bf16[8,128,128]{2,1,0:T(8,128)(2,1)S(1)}, u32[]{:S(2)}, u32[]{:S(2)}) collective-permute-start(bf16[8,128,128]{2,1,0:T(8,128)(2,1)S(1)} %slice.9.q_own_ref), channel_id=1, source_target_pairs={{0,8},{8,0},{1,9},{9,1},{2,10},{10,2},{3,11},{11,3},{4,12},{12,4},... | collective-permute-start | bytes 786440 | tf_op jit(solution)/shard_map/ppermute | solution.py:389
  37.7 0.7 copy-start.3
  38.5 13.6 %copy-start.1 = (s32[35]{0:T(128)}, s32[35]{0:T(128)S(1)}, u32[]{:S(2)}) copy-start(s32[35]{0:T(128)S(1)} %pad_add_fusion.int_ref) | copy-start | bytes 424
  38.5 13.6 %collective-permute-start.2 = (bf16[8,256,128]{2,1,0:T(8,128)(2,1)S(1)}, bf16[8,256,128]{2,1,0:T(8,128)(2,1)S(1)}, u32[]{:S(2)}, u32[]{:S(2)}) collective-permute-start(bf16[8,256,128]{2,1,0:T(8,128)(2,1)S(1)} %slice.8.own_ref), channel_id=1, source_target_pairs={{0,256},{1,257},{2,258},{3,259},{4,260},{5,261},{6,262},{7,263},{8... | collective-permute-start | bytes 1572872 | tf_op jit(solution)/shard_map/ppermute | solution.py:390
  45.1 7.0 %collective-permute-start.3 = (bf16[8,256,128]{2,1,0:T(8,128)(2,1)S(1)}, bf16[8,256,128]{2,1,0:T(8,128)(2,1)S(1)}, u32[]{:S(2)}, u32[]{:S(2)}) collective-permute-start(bf16[8,256,128]{2,1,0:T(8,128)(2,1)S(1)} %collective-permute-done.pair_ref), channel_id=1, source_target_pairs={{0,256},{1,257},{2,258},{3,259},{4,260},{5,261},{6,262},{7,263},{8... | collective-permute-start | bytes 1572872 | tf_op jit(solution)/shard_map/ppermute | solution.py:392
  57.5 0.7 copy-start
  58.2 9.4 %collective-permute-start.4 = (bf16[8,144,128]{2,1,0:T(8,128)(2,1)S(1)}, bf16[8,144,128]{2,1,0:T(8,128)(2,1)S(1)}, u32[]{:S(2)}, u32[]{:S(2)}) collective-permute-start(bf16[8,144,128]{2,1,0:T(8,128)(2,1)S(1)} %get-tuple-element.18), channel_id=1, source_target_pairs={{0,8},{8,0},{1,9},{9,1},{2,10},{10,2},{3,11},{11,3},{4,12},{12,4},... | collective-permute-start | bytes 884744 | tf_op jit(solution)/shard_map/ppermute | solution.py:395
  67.6 0.7 copy-start.2

commit v3 on v1

--- a/solution.py
+++ b/solution.py
@@ -50,17 +50,17 @@
     for h in range(HEADS):
         logs = []
         for n in range(2):
-            terms = in_ref[h, n, ROWS:, :].astype(jnp.float32)
+            terms = in_ref[n, h, ROWS:, :].astype(jnp.float32)
             logs.append(terms[0:1] + terms[1:2] + terms[2:3])
         top = jnp.maximum(logs[0], logs[1])
         a, b = jnp.exp2(logs[0] - top), jnp.exp2(logs[1] - top)
-        o = in_ref[h, 0, :ROWS, :].astype(jnp.float32) * (a / (a + b))
-        o += in_ref[h, 1, :ROWS, :].astype(jnp.float32) * (b / (a + b))
+        o = in_ref[0, h, :ROWS, :].astype(jnp.float32) * (a / (a + b))
+        o += in_ref[1, h, :ROWS, :].astype(jnp.float32) * (b / (a + b))
         out_ref[:, h * HEAD_DIM : (h + 1) * HEAD_DIM] = o.T.astype(jnp.bfloat16)
 
 
 def combine(parts):
-    shape = (HEADS, 2, ROWS + STATS, HEAD_DIM)
+    shape = (2, HEADS, ROWS + STATS, HEAD_DIM)
     return pl.pallas_call(
         combine_kernel,
         grid=(1,),
@@ -101,7 +101,7 @@
 
 
 def key_places(x):
-    row = lax.broadcasted_iota(jnp.int32, (HALF, TILE), 0)
+    row = lax.broadcasted_iota(jnp.int32, (HALF, HALF), 0)
     return jnp.where(row < ROWS, x, X - 1 - x) * ROWS + (row & (ROWS - 1))
 
 
@@ -112,29 +112,46 @@
     )
 
 
-def scores_of(refs, s_ref, q, g, n, m, kept):
-    part = slice(n * HALF, (n + 1) * HALF)
+def piece(n):
+    return slice(n * HALF, (n + 1) * HALF)
+
+
+def scores_of(refs, s_ref, q, g, n, m, kept, c):
     k = jnp.concatenate([ref[2 * g + n, :ROWS, :] for ref in refs], axis=0)
-    s = jnp.dot(k, q, preferred_element_type=jnp.float32)
+    s = jnp.dot(k, q[:, piece(c)], preferred_element_type=jnp.float32)
     if kept is not None:
         s = jnp.where(kept, s, NEG)
-    s_ref[g, part, :] = s
-    return jnp.maximum(m, jnp.max(s.reshape(HALF // 8, 8, TILE), axis=0))
-
-
-def mix(refs, s_ref, g, n, shift, l, acc):
-    part = slice(n * HALF, (n + 1) * HALF)
-    p = jnp.exp2(s_ref[g, part, :] * C - shift)
-    l = l + jnp.sum(p.reshape(HALF // 8, 8, TILE), axis=0)
+    s_ref[g, piece(n), piece(c)] = s
+    return jnp.maximum(m, jnp.max(s.reshape(HALF // 8, 8, HALF), axis=0))
+
+
+def mix(refs, s_ref, g, n, c, shift, l, acc):
+    p = jnp.exp2(s_ref[g, piece(n), piece(c)] * C - shift[:, piece(c)])
+    l = l + jnp.sum(p.reshape(HALF // 8, 8, HALF), axis=0)
     vt = jnp.concatenate([ref[2 * g + n, ROWS:, :] for ref in refs], axis=1)
     acc = acc + jnp.dot(vt, p.astype(jnp.bfloat16), preferred_element_type=jnp.float32)
     return l, acc
 
 
 def mix_block(refs, s_ref, g, shift, l, acc):
+    l, acc = list(l), list(acc)
     for n in range(2):
-        l, acc = mix(refs, s_ref, g, n, shift, l, acc)
-    return l, acc
+        for c in range(2):
+            l[c], acc[c] = mix(refs, s_ref, g, n, c, shift, l[c], acc[c])
+    return tuple(l), tuple(acc)
+
+
+def sums_and_scores(refs, s_ref, g, shift, score, m, l, acc):
+    m, l, acc = list(m), list(l), list(acc)
+    for n in range(2):
+        for c in range(2):
+            l[c], acc[c] = mix(refs, s_ref, g, n, c, shift, l[c], acc[c])
+            m[c] = score(n, c, m[c])
+    return tuple(m), tuple(l), tuple(acc)
+
+
+def joined(parts):
+    return jnp.concatenate(parts, axis=1)
 
 
 def shift_of(top):
@@ -164,39 +181,38 @@
         refs = (own_ref, pair_ref)
         key_rows = key_places(x)
 
-        def score(s_ref, i, q, g, n, m, masked, diagonal):
+        def score(s_ref, i, q, g, masked, diagonal, n, c, m):
             kept = None
             if masked:
-                kept = key_rows >= first_ref[i : i + 1, :] - (g * WIDE + n * SPAN)
+                kept = key_rows >= first_ref[i : i + 1, piece(c)] - (g * WIDE + n * SPAN)
                 if diagonal:
-                    kept &= key_rows <= places(x, (1, TILE)) - n * SPAN
-            return scores_of(refs, s_ref, q, g, n, m, kept)
+                    kept &= key_rows <= places(x, (1, TILE))[:, piece(c)] - n * SPAN
+            return scores_of(refs, s_ref, q, g, n, m, kept, c)
 
         def score_diagonal(s_ref, i, q, m):
+            m = list(m)
             for n in range(2):
-                m = score(s_ref, i, q, i, n, m, True, True)
-            return m
-
-        none = jnp.full((8, TILE), NEG, jnp.float32)
-        zeros = jnp.zeros((8, TILE), jnp.float32)
+                for c in range(2):
+                    m[c] = score(s_ref, i, q, i, True, True, n, c, m[c])
+            return tuple(m)
+
+        none = (jnp.full((8, HALF), NEG, jnp.float32),) * 2
+        zeros = (jnp.zeros((8, HALF), jnp.float32),) * 2
         buffers = (even_ref, odd_ref)
         q = load_queries(q_own_ref, q_pair_ref, 0)
         m = score_diagonal(even_ref, 0, q, none)
         for i in range(TILES):
             s_ref, later_ref = buffers[i % 2], buffers[(i + 1) % 2]
-            top = jnp.max(m, axis=0, keepdims=True)
+            top = jnp.max(joined(m), axis=0, keepdims=True)
             shift = shift_of(top)
             begin = jnp.maximum(lo_ref[i], 0)
-            sums = (zeros, jnp.zeros((HEAD_DIM, TILE), jnp.float32))
+            sums = (zeros, (jnp.zeros((HEAD_DIM, HALF), jnp.float32),) * 2)
             if i + 1 < TILES:
                 q = load_queries(q_own_ref, q_pair_ref, i + 1)
 
                 def step(masked, g, carry, i=i, q=q, shift=shift, s_ref=s_ref, later_ref=later_ref):
-                    m, l, acc = carry
-                    for n in range(2):
-                        l, acc = mix(refs, s_ref, g, n, shift, l, acc)
-                        m = score(later_ref, i + 1, q, g, n, m, masked, False)
-                    return m, l, acc
+                    later = functools.partial(score, later_ref, i + 1, q, g, masked, False)
+                    return sums_and_scores(refs, s_ref, g, shift, later, *carry)
 
                 carry = (none,) + sums
                 if i > 0:
@@ -212,9 +228,9 @@
                     lambda g, c, s_ref=s_ref, shift=shift: mix_block(refs, s_ref, g, shift, *c),
                     sums,
                 )
-            l = jnp.sum(l, axis=0, keepdims=True)
+            l = jnp.sum(joined(l), axis=0, keepdims=True)
             row = lax.broadcasted_iota(jnp.int32, (8, TILE), 0)
-            acc_ref[i] = acc
+            acc_ref[i] = joined(acc)
             state_ref[i] = jnp.where(row == 0, l, top)
 
 
@@ -237,7 +253,9 @@
 
     @pl.when(slot < HEADS)
     def _():
-        find_documents(blk, x, int_ref, first_ref, lo_ref, hi_ref)
+        @pl.when(blk > 0)
+        def _():
+            find_documents(blk, x, int_ref, first_ref, lo_ref, hi_ref)
 
         def begin_of(i):
             return jnp.where(blk > 0, jnp.clip(lo_ref[i] + TILES, 0, TILES), TILES)
@@ -245,22 +263,25 @@
         refs = (prev_own_ref, prev_pair_ref)
         key_rows = key_places(x)
 
-        def score(s_ref, i, q, g, n, m, masked):
+        def score(s_ref, i, q, g, masked, n, c, m):
             kept = None
             if masked:
-                kept = key_rows >= first_ref[i : i + 1, :] - ((g - TILES) * WIDE + n * SPAN)
-            return scores_of(refs, s_ref, q, g, n, m, kept)
+                start = first_ref[i : i + 1, piece(c)] - ((g - TILES) * WIDE + n * SPAN)
+                kept = key_rows >= start
+            return scores_of(refs, s_ref, q, g, n, m, kept, c)
 
         def score_first(masked, g, m):
+            m = list(m)
             for n in range(2):
-                m = score(even_ref, 0, q, g, n, m, masked)
-            return m
+                for c in range(2):
+                    m[c] = score(even_ref, 0, q, g, masked, n, c, m[c])
+            return tuple(m)
 
         def middle_of(i, begin):
             return jnp.clip(hi_ref[i] + TILES + 1, begin, TILES)
 
-        none = jnp.full((8, TILE), NEG, jnp.float32)
-        zeros = jnp.zeros((8, TILE), jnp.float32)
+        none = (jnp.full((8, HALF), NEG, jnp.float32),) * 2
+        zeros = (jnp.zeros((8, HALF), jnp.float32),) * 2
         buffers = (even_ref, odd_ref)
         q = load_queries(q_own_ref, q_pair_ref, 0)
         begin = begin_of(0)
@@ -270,20 +291,18 @@
         for i in range(TILES):
             s_ref, later_ref = buffers[i % 2], buffers[(i + 1) % 2]
             own_l, own_top = state_ref[i, 0:1, :], state_ref[i, 1:2, :]
-            top = jnp.maximum(jnp.max(m, axis=0, keepdims=True), own_top)
+            top = jnp.maximum(jnp.max(joined(m), axis=0, keepdims=True), own_top)
             shift = shift_of(top)
             scale = jnp.where(own_top > 0.5 * NEG, jnp.exp2(own_top * C - shift), 0.0)
             begin = begin_of(i)
-            sums = (zeros, acc_ref[i] * scale)
+            scaled = acc_ref[i] * scale
+            sums = (zeros, (scaled[:, piece(0)], scaled[:, piece(1)]))
             if i + 1 < TILES:
                 q = load_queries(q_own_ref, q_pair_ref, i + 1)
 
                 def step(masked, g, carry, i=i, q=q, shift=shift, s_ref=s_ref, later_ref=later_ref):
-                    m, l, acc = carry
-                    for n in range(2):
-                        l, acc = mix(refs, s_ref, g, n, shift, l, acc)
-                        m = score(later_ref, i + 1, q, g, n, m, masked)
-                    return m, l, acc
+                    later = functools.partial(score, later_ref, i + 1, q, g, masked)
+                    return sums_and_scores(refs, s_ref, g, shift, later, *carry)
 
                 middle = middle_of(i + 1, begin)
                 carry = (none,) + sums
@@ -296,10 +315,10 @@
                     lambda g, c, s_ref=s_ref, shift=shift: mix_block(refs, s_ref, g, shift, *c),
                     sums,
                 )
-            l = jnp.sum(l, axis=0, keepdims=True) + own_l * scale
+            l = jnp.sum(joined(l), axis=0, keepdims=True) + own_l * scale
             some = l > 0.0
             l = jnp.where(some, l, 1.0)
-            o = (acc * (1.0 / l)).astype(jnp.bfloat16)
+            o = (joined(acc) * (1.0 / l)).astype(jnp.bfloat16)
             log = jnp.where(some, shift + jnp.log(l) * LOG2E, NEG)
             high = log.astype(jnp.bfloat16).astype(jnp.float32)
             middle = (log - high).astype(jnp.bfloat16).astype(jnp.float32)
@@ -310,8 +329,8 @@
             for n in range(4):
                 part = slice(n * ROWS, (n + 1) * ROWS)
                 y, to = 2 * i + (n & 1), (x & 1) ^ (n >> 1)
-                o_ref[y, to, :ROWS, :] = o[:, part]
-                o_ref[y, to, ROWS:, :] = stats[:, part]
+                o_ref[to, y, :ROWS, :] = o[:, part]
+                o_ref[to, y, ROWS:, :] = stats[:, part]
 
 
 SCRATCH = [
@@ -347,7 +366,7 @@
 def attend_prev(ints, q_own, q_pair, prev_own, prev_pair, acc, state):
     return pl.pallas_call(
         prev_kernel,
-        out_shape=jax.ShapeDtypeStruct((Y, 2, ROWS + STATS, HEAD_DIM), jnp.bfloat16),
+        out_shape=jax.ShapeDtypeStruct((2, Y, ROWS + STATS, HEAD_DIM), jnp.bfloat16),
         in_specs=[SMEM] + [VMEM] * 6,
         out_specs=VMEM,
         scratch_shapes=SCRATCH,
@@ -373,8 +392,8 @@
     state = attend_own(ints, own_queries, pair_queries, own, pair)
     parts = attend_prev(ints, own_queries, pair_queries, prev_own, prev_pair, *state)
     parts = parts.reshape(2 * Y, ROWS + STATS, HEAD_DIM)
-    parts = lax.all_to_all(parts, ("y", "xl"), 0, 0, tiled=True)
-    return combine(parts.reshape(Y, 2, ROWS + STATS, HEAD_DIM))
+    parts = lax.all_to_all(parts, ("xl", "y"), 0, 0, tiled=True)
+    return combine(parts.reshape(2, Y, ROWS + STATS, HEAD_DIM))
 
 
 def solution(mesh):

time: 81.9 us -> 79.6 us (0.972)
  Pallas kernels: 15.2 us -> 12.5 us
    pallas_call x1, Pallas kernels: 6.25 us -> 3.18 us  [attend_prev(): pl.pallas_call(prev_kernel, out_shape=jax.ShapeDtypeStruct((2, Y, ROWS +...]
  transfers between devices with their start and end apart: 4 -> 4, of which waited for: 2 -> 2; matrix products, arithmetic and copies ran while one was open for 0% -> 0% of each run, Pallas kernels for 6% -> 7%
where the time goes in v3:
time: 79.6 us; the launch traced here: 79.2 us
  blocking collectives  50 us (63%)
  Pallas kernels  12.5 us (16%)
  starting transfers between devices  10.5 us (13%)
  waiting for transfers between devices  5.31 us (7%)
    all_to_all x1, blocking collectives, body(): got = lax.all_to_all(pack(queries, keys, values), 'y', 0, 0, tiled=True)  27.6 us
    all_to_all x1, blocking collectives, body(): parts = lax.all_to_all(parts, ('xl', 'y'), 0, 0, tiled=True)  22.3 us
    ppermute x1, starting transfers between devices, body(): pair = lax.ppermute(own, ('xh', 'xl'), KEY_PAIRS)  6.03 us
    pallas_call x1, Pallas kernels, attend_own(): pl.pallas_call(own_kernel, out_shape=(jax.ShapeDtypeStruct(ACC, jnp.float...  5.44 us
    ppermute x1, waiting for transfers between devices, body(): pair_queries = lax.ppermute(own_queries, 'xl', QUERY_PAIRS)  3.45 us
    pallas_call x1, Pallas kernels, attend_prev(): pl.pallas_call(prev_kernel, out_shape=jax.ShapeDtypeStruct((2, Y, ROWS +...  3.18 us
    pallas_call x1, Pallas kernels, pack(): pl.pallas_call(pack_kernel, out_shape=jax.ShapeDtypeStruct((Y, 2 * ROWS +...  2.11 us
    ppermute x1, starting transfers between devices, body(): pair_queries = lax.ppermute(own_queries, 'xl', QUERY_PAIRS)  1.92 us
  transfers between devices with their start and end apart: 4, of which 2 were waited for; matrix products, arithmetic and copies ran while one was open for 0% of the time, Pallas kernels for 7%

profile of v3, /device:TPU:1, one launch (start us, length us, event | category | flops | bytes accessed | tf_op | source)
XLA Modules:
  0.0 79.2 jit_solution(7886002005764302571)
XLA Ops:
  0.0 2.1 %pack.1 = bf16[8,384,128]{2,1,0:T(8,128)(2,1)} custom-call(bf16[128,640]{1,0:T(8,128)(2,1)} %q_ref.1, bf16[128,640]{1,0:T(8,128)(2,1)} %k_ref.1, bf16[128,640]{1,0:T(8,128)(2,1)} %v_ref.1), custom_call_target="tpu_custom_call" | custom-call | tf_op jit(solution)/shard_map/pack/pallas_call | solution.py:42
  2.1 27.6 %all_to_all.10 = bf16[8,384,128]{2,1,0:T(8,128)(2,1)S(1)} all-to-all(bf16[8,384,128]{2,1,0:T(8,128)(2,1)} %pack.1), channel_id=1, replica_groups=mesh['blk'=2,'y'=8,'xh'=2,'xl'=2,'tp'=8] {'y'}, dimensions={0} | all-to-all | bytes 1572864 | tf_op jit(solution)/shard_map/all_to_all | solution.py:385
  29.8 6.0 %collective-permute-start = (bf16[8,256,128]{2,1,0:T(8,128)(2,1)S(1)}, bf16[8,256,128]{2,1,0:T(8,128)(2,1)S(1)}, u32[]{:S(2)}, u32[]{:S(2)}) collective-permute-start(bf16[8,256,128]{2,1,0:T(8,128)(2,1)S(1)} %slice.8.own_ref), channel_id=1, source_target_pairs={{0,24},{8,16},{16,8},{24,0},{1,25},{9,17},{17,9},{25,1},{2,26},{10... | collective-permute-start | bytes 1572872 | tf_op jit(solution)/shard_map/ppermute | solution.py:387
  35.8 1.9 %collective-permute-start.1 = (bf16[8,128,128]{2,1,0:T(8,128)(2,1)S(1)}, bf16[8,128,128]{2,1,0:T(8,128)(2,1)S(1)}, u32[]{:S(2)}, u32[]{:S(2)}) collective-permute-start(bf16[8,128,128]{2,1,0:T(8,128)(2,1)S(1)} %slice.9.q_own_ref), channel_id=1, source_target_pairs={{0,8},{8,0},{1,9},{9,1},{2,10},{10,2},{3,11},{11,3},{4,12},{12,4},... | collective-permute-start | bytes 786440 | tf_op jit(solution)/shard_map/ppermute | solution.py:388
  37.8 0.0 copy-start
  37.8 0.6 copy-done
  38.4 0.1 pad_add_fusion.int_ref
  38.5 1.3 %collective-permute-start.2 = (bf16[8,256,128]{2,1,0:T(8,128)(2,1)S(1)}, bf16[8,256,128]{2,1,0:T(8,128)(2,1)S(1)}, u32[]{:S(2)}, u32[]{:S(2)}) collective-permute-start(bf16[8,256,128]{2,1,0:T(8,128)(2,1)S(1)} %slice.8.own_ref), channel_id=1, source_target_pairs={{0,256},{1,257},{2,258},{3,259},{4,260},{5,261},{6,262},{7,263},{8... | collective-permute-start | bytes 1572872 | tf_op jit(solution)/shard_map/ppermute | solution.py:389
  39.8 3.4 %collective-permute-done.1.q_pair_ref = bf16[8,128,128]{2,1,0:T(8,128)(2,1)S(1)} collective-permute-done((bf16[8,128,128]{2,1,0:T(8,128)(2,1)S(1)}, bf16[8,128,128]{2,1,0:T(8,128)(2,1)S(1)}, u32[]{:S(2)}, u32[]{:S(2)}) %collective-permute-start.1) | collective-permute-done | bytes 262176 | tf_op jit(solution)/shard_map/ppermute | solution.py:388
  43.2 1.9 %collective-permute-done.pair_ref = bf16[8,256,128]{2,1,0:T(8,128)(2,1)S(1)} collective-permute-done((bf16[8,256,128]{2,1,0:T(8,128)(2,1)S(1)}, bf16[8,256,128]{2,1,0:T(8,128)(2,1)S(1)}, u32[]{:S(2)}, u32[]{:S(2)}) %collective-permute-start) | collective-permute-done | bytes 524320 | tf_op jit(solution)/shard_map/ppermute | solution.py:387
  45.1 1.3 %collective-permute-start.3 = (bf16[8,256,128]{2,1,0:T(8,128)(2,1)S(1)}, bf16[8,256,128]{2,1,0:T(8,128)(2,1)S(1)}, u32[]{:S(2)}, u32[]{:S(2)}) collective-permute-start(bf16[8,256,128]{2,1,0:T(8,128)(2,1)S(1)} %collective-permute-done.pair_ref), channel_id=1, source_target_pairs={{0,256},{1,257},{2,258},{3,259},{4,260},{5,261},{6,262},{7,263},{8... | collective-permute-start | bytes 1572872 | tf_op jit(solution)/shard_map/ppermute | solution.py:391
  46.4 5.4 %attend_own.1 = (f32[4,128,512]{2,1,0:T(8,128)S(1)}, f32[4,8,512]{2,1,0:T(8,128)S(1)}) custom-call(s32[35]{0:T(128)S(1)} %pad_add_fusion.int_ref, bf16[8,128,128]{2,1,0:T(8,128)(2,1)S(1)} %slice.9.q_own_ref, bf16[8,128,128]{2,1,0:T(8,128)(2,1)S(1)} %collective-permute-done.1.q_pair_ref, bf16[8,256,128]{2,1,0:T(8,128)(2,1)S(1)} %slice.8.own_ref, ...), custom_call_target="tpu_custom_call" | custom-call | flops 1073741824 | bytes 4194304 | tf_op jit(solution)/shard_map/attend_own/pallas_call | solution.py:349
  51.8 0.0 collective-permute-done.2.prev_own_ref
  51.8 0.0 collective-permute-done.3.prev_pair_ref
  51.9 3.2 %attend_prev.1 = bf16[2,8,144,128]{3,2,1,0:T(8,128)(2,1)S(1)} custom-call(s32[35]{0:T(128)S(1)} %pad_add_fusion.int_ref, bf16[8,128,128]{2,1,0:T(8,128)(2,1)S(1)} %slice.9.q_own_ref, bf16[8,128,128]{2,1,0:T(8,128)(2,1)S(1)} %collective-permute-done.1.q_pair_ref, bf16[8,256,128]{2,1,0:T(8,128)(2,1)S(1)} %collective-permute-done.2.prev_own_ref, ...), custom_call_target="tpu_custom_call" | custom-call | flops 536870912 | bytes 4194304 | tf_op jit(solution)/shard_map/attend_prev/pallas_call | solution.py:367
  55.0 22.3 %all_to_all.11 = bf16[16,144,128]{2,1,0:T(8,128)(2,1)} all-to-all(bf16[16,144,128]{2,1,0:T(8,128)(2,1)S(1)} %bitcast.5), channel_id=1, replica_groups=mesh['blk'=2,'y'=8,'xh'=2,'xl'=2,'tp'=8] {'xl','y'}, dimensions={0} | all-to-all | bytes 1179648 | tf_op jit(solution)/shard_map/all_to_all | solution.py:395
  77.4 1.8 %combine.1 = bf16[128,640]{1,0:T(8,128)(2,1)} custom-call(bf16[2,8,144,128]{3,2,1,0:T(8,128)(2,1)} %bitcast.6), custom_call_target="tpu_custom_call" | custom-call | tf_op jit(solution)/shard_map/combine/pallas_call | solution.py:64
  (2 shorter events, 0.1 us)
Async XLA Ops:
  29.8 15.3 %collective-permute-start = (bf16[8,256,128]{2,1,0:T(8,128)(2,1)S(1)}, bf16[8,256,128]{2,1,0:T(8,128)(2,1)S(1)}, u32[]{:S(2)}, u32[]{:S(2)}) collective-permute-start(bf16[8,256,128]{2,1,0:T(8,128)(2,1)S(1)} %slice.8.own_ref), channel_id=1, source_target_pairs={{0,24},{8,16},{16,8},{24,0},{1,25},{9,17},{17,9},{25,1},{2,26},{10... | collective-permute-start | bytes 1572872 | tf_op jit(solution)/shard_map/ppermute | solution.py:387
  35.8 7.4 %collective-permute-start.1 = (bf16[8,128,128]{2,1,0:T(8,128)(2,1)S(1)}, bf16[8,128,128]{2,1,0:T(8,128)(2,1)S(1)}, u32[]{:S(2)}, u32[]{:S(2)}) collective-permute-start(bf16[8,128,128]{2,1,0:T(8,128)(2,1)S(1)} %slice.9.q_own_ref), channel_id=1, source_target_pairs={{0,8},{8,0},{1,9},{9,1},{2,10},{10,2},{3,11},{11,3},{4,12},{12,4},... | collective-permute-start | bytes 786440 | tf_op jit(solution)/shard_map/ppermute | solution.py:388
  37.8 0.7 copy-start
  38.5 13.3 %collective-permute-start.2 = (bf16[8,256,128]{2,1,0:T(8,128)(2,1)S(1)}, bf16[8,256,128]{2,1,0:T(8,128)(2,1)S(1)}, u32[]{:S(2)}, u32[]{:S(2)}) collective-permute-start(bf16[8,256,128]{2,1,0:T(8,128)(2,1)S(1)} %slice.8.own_ref), channel_id=1, source_target_pairs={{0,256},{1,257},{2,258},{3,259},{4,260},{5,261},{6,262},{7,263},{8... | collective-permute-start | bytes 1572872 | tf_op jit(solution)/shard_map/ppermute | solution.py:389
  45.1 6.8 %collective-permute-start.3 = (bf16[8,256,128]{2,1,0:T(8,128)(2,1)S(1)}, bf16[8,256,128]{2,1,0:T(8,128)(2,1)S(1)}, u32[]{:S(2)}, u32[]{:S(2)}) collective-permute-start(bf16[8,256,128]{2,1,0:T(8,128)(2,1)S(1)} %collective-permute-done.pair_ref), channel_id=1, source_target_pairs={{0,256},{1,257},{2,258},{3,259},{4,260},{5,261},{6,262},{7,263},{8... | collective-permute-start | bytes 1572872 | tf_op jit(solution)/shard_map/ppermute | solution.py:391

commit v4 on v3

--- a/solution.py
+++ b/solution.py
@@ -60,13 +60,10 @@
 
 
 def combine(parts):
-    shape = (2, HEADS, ROWS + STATS, HEAD_DIM)
     return pl.pallas_call(
         combine_kernel,
-        grid=(1,),
         out_shape=jax.ShapeDtypeStruct((ROWS, HEADS * HEAD_DIM), jnp.bfloat16),
-        in_specs=[pl.BlockSpec(shape, lambda i: (0, 0, 0, 0))],
-        out_specs=pl.BlockSpec((ROWS, HEADS * HEAD_DIM), lambda i: (0, 0)),
+        in_specs=[pl.BlockSpec(memory_space=pltpu.VMEM)],
         name="combine",
     )(parts)
 
@@ -368,7 +365,6 @@
         prev_kernel,
         out_shape=jax.ShapeDtypeStruct((2, Y, ROWS + STATS, HEAD_DIM), jnp.bfloat16),
         in_specs=[SMEM] + [VMEM] * 6,
-        out_specs=VMEM,
         scratch_shapes=SCRATCH,
         compiler_params=pltpu.CompilerParams(vmem_limit_bytes=16 << 20),
         cost_estimate=pl.CostEstimate(

time: 79.6 us -> 81.1 us (1.019)
  Pallas kernels: 12.5 us -> 14.6 us
    pallas_call x1, Pallas kernels: 3.18 us -> 5.84 us  [attend_prev(): pl.pallas_call(prev_kernel, out_shape=jax.ShapeDtypeStruct((2, Y, ROWS +...]
  transfers between devices with their start and end apart: 4 -> 4, of which waited for: 2 -> 3; matrix products, arithmetic and copies ran while one was open for 0% -> 0% of each run, Pallas kernels for 7% -> 6%
where the time goes in v4:
time: 81.1 us; the launch traced here: 80.7 us
  blocking collectives  49.3 us (61%)
  Pallas kernels  14.6 us (18%)
  starting transfers between devices  10.5 us (13%)
  waiting for transfers between devices  5.52 us (7%)
    all_to_all x1, blocking collectives, body(): got = lax.all_to_all(pack(queries, keys, values), 'y', 0, 0, tiled=True)  27.6 us
    all_to_all x1, blocking collectives, body(): parts = lax.all_to_all(parts, ('xl', 'y'), 0, 0, tiled=True)  21.6 us
    ppermute x1, starting transfers between devices, body(): pair = lax.ppermute(own, ('xh', 'xl'), KEY_PAIRS)  6.03 us
    pallas_call x1, Pallas kernels, attend_prev(): pl.pallas_call(prev_kernel, out_shape=jax.ShapeDtypeStruct((2, Y, ROWS +...  5.84 us
    pallas_call x1, Pallas kernels, attend_own(): pl.pallas_call(own_kernel, out_shape=(jax.ShapeDtypeStruct(ACC, jnp.float...  4.72 us
    ppermute x1, waiting for transfers between devices, body(): pair_queries = lax.ppermute(own_queries, 'xl', QUERY_PAIRS)  3.45 us
    pallas_call x1, Pallas kernels, pack(): pl.pallas_call(pack_kernel, out_shape=jax.ShapeDtypeStruct((Y, 2 * ROWS +...  2.11 us
    ppermute x1, starting transfers between devices, body(): pair_queries = lax.ppermute(own_queries, 'xl', QUERY_PAIRS)  1.92 us
  transfers between devices with their start and end apart: 4, of which 3 were waited for; matrix products, arithmetic and copies ran while one was open for 0% of the time, Pallas kernels for 6%

profile of v4, /device:TPU:1, one launch (start us, length us, event | category | flops | bytes accessed | tf_op | source)
XLA Modules:
  0.0 80.7 jit_solution(2125853242284833892)
XLA Ops:
  0.0 2.1 %pack.1 = bf16[8,384,128]{2,1,0:T(8,128)(2,1)} custom-call(bf16[128,640]{1,0:T(8,128)(2,1)} %q_ref.1, bf16[128,640]{1,0:T(8,128)(2,1)} %k_ref.1, bf16[128,640]{1,0:T(8,128)(2,1)} %v_ref.1), custom_call_target="tpu_custom_call" | custom-call | tf_op jit(solution)/shard_map/pack/pallas_call | solution.py:42
  2.1 27.6 %all_to_all.10 = bf16[8,384,128]{2,1,0:T(8,128)(2,1)S(1)} all-to-all(bf16[8,384,128]{2,1,0:T(8,128)(2,1)} %pack.1), channel_id=1, replica_groups=mesh['blk'=2,'y'=8,'xh'=2,'xl'=2,'tp'=8] {'y'}, dimensions={0} | all-to-all | bytes 1572864 | tf_op jit(solution)/shard_map/all_to_all | solution.py:381
  29.8 6.0 %collective-permute-start = (bf16[8,256,128]{2,1,0:T(8,128)(2,1)S(1)}, bf16[8,256,128]{2,1,0:T(8,128)(2,1)S(1)}, u32[]{:S(2)}, u32[]{:S(2)}) collective-permute-start(bf16[8,256,128]{2,1,0:T(8,128)(2,1)S(1)} %slice.8.own_ref), channel_id=1, source_target_pairs={{0,24},{8,16},{16,8},{24,0},{1,25},{9,17},{17,9},{25,1},{2,26},{10... | collective-permute-start | bytes 1572872 | tf_op jit(solution)/shard_map/ppermute | solution.py:383
  35.8 1.9 %collective-permute-start.1 = (bf16[8,128,128]{2,1,0:T(8,128)(2,1)S(1)}, bf16[8,128,128]{2,1,0:T(8,128)(2,1)S(1)}, u32[]{:S(2)}, u32[]{:S(2)}) collective-permute-start(bf16[8,128,128]{2,1,0:T(8,128)(2,1)S(1)} %slice.9.q_own_ref), channel_id=1, source_target_pairs={{0,8},{8,0},{1,9},{9,1},{2,10},{10,2},{3,11},{11,3},{4,12},{12,4},... | collective-permute-start | bytes 786440 | tf_op jit(solution)/shard_map/ppermute | solution.py:384
  37.8 0.0 copy-start
  37.8 0.6 copy-done
  38.4 0.1 pad_add_fusion.int_ref
  38.5 1.3 %collective-permute-start.2 = (bf16[8,256,128]{2,1,0:T(8,128)(2,1)S(1)}, bf16[8,256,128]{2,1,0:T(8,128)(2,1)S(1)}, u32[]{:S(2)}, u32[]{:S(2)}) collective-permute-start(bf16[8,256,128]{2,1,0:T(8,128)(2,1)S(1)} %slice.8.own_ref), channel_id=1, source_target_pairs={{0,256},{1,257},{2,258},{3,259},{4,260},{5,261},{6,262},{7,263},{8... | collective-permute-start | bytes 1572872 | tf_op jit(solution)/shard_map/ppermute | solution.py:385
  39.8 3.4 %collective-permute-done.1.q_pair_ref = bf16[8,128,128]{2,1,0:T(8,128)(2,1)S(1)} collective-permute-done((bf16[8,128,128]{2,1,0:T(8,128)(2,1)S(1)}, bf16[8,128,128]{2,1,0:T(8,128)(2,1)S(1)}, u32[]{:S(2)}, u32[]{:S(2)}) %collective-permute-start.1) | collective-permute-done | bytes 262176 | tf_op jit(solution)/shard_map/ppermute | solution.py:384
  43.2 1.9 %collective-permute-done.pair_ref = bf16[8,256,128]{2,1,0:T(8,128)(2,1)S(1)} collective-permute-done((bf16[8,256,128]{2,1,0:T(8,128)(2,1)S(1)}, bf16[8,256,128]{2,1,0:T(8,128)(2,1)S(1)}, u32[]{:S(2)}, u32[]{:S(2)}) %collective-permute-start) | collective-permute-done | bytes 524320 | tf_op jit(solution)/shard_map/ppermute | solution.py:383
  45.1 1.3 %collective-permute-start.3 = (bf16[8,256,128]{2,1,0:T(8,128)(2,1)S(1)}, bf16[8,256,128]{2,1,0:T(8,128)(2,1)S(1)}, u32[]{:S(2)}, u32[]{:S(2)}) collective-permute-start(bf16[8,256,128]{2,1,0:T(8,128)(2,1)S(1)} %collective-permute-done.pair_ref), channel_id=1, source_target_pairs={{0,256},{1,257},{2,258},{3,259},{4,260},{5,261},{6,262},{7,263},{8... | collective-permute-start | bytes 1572872 | tf_op jit(solution)/shard_map/ppermute | solution.py:387
  46.4 4.7 %attend_own.1 = (f32[4,128,512]{2,1,0:T(8,128)S(1)}, f32[4,8,512]{2,1,0:T(8,128)S(1)}) custom-call(s32[35]{0:T(128)S(1)} %pad_add_fusion.int_ref, bf16[8,128,128]{2,1,0:T(8,128)(2,1)S(1)} %slice.9.q_own_ref, bf16[8,128,128]{2,1,0:T(8,128)(2,1)S(1)} %collective-permute-done.1.q_pair_ref, bf16[8,256,128]{2,1,0:T(8,128)(2,1)S(1)} %slice.8.own_ref, ...), custom_call_target="tpu_custom_call" | custom-call | flops 1073741824 | bytes 4194304 | tf_op jit(solution)/shard_map/attend_own/pallas_call | solution.py:346
  51.1 0.0 collective-permute-done.2.prev_own_ref
  51.1 0.2 collective-permute-done.3.prev_pair_ref
  51.3 5.8 %attend_prev.1 = bf16[2,8,144,128]{3,2,1,0:T(8,128)(2,1)S(1)} custom-call(s32[35]{0:T(128)S(1)} %pad_add_fusion.int_ref, bf16[8,128,128]{2,1,0:T(8,128)(2,1)S(1)} %slice.9.q_own_ref, bf16[8,128,128]{2,1,0:T(8,128)(2,1)S(1)} %collective-permute-done.1.q_pair_ref, bf16[8,256,128]{2,1,0:T(8,128)(2,1)S(1)} %collective-permute-done.2.prev_own_ref, ...), custom_call_target="tpu_custom_call" | custom-call | flops 536870912 | bytes 4194304 | tf_op jit(solution)/shard_map/attend_prev/pallas_call | solution.py:364
  57.2 21.6 %all_to_all.11 = bf16[16,144,128]{2,1,0:T(8,128)(2,1)} all-to-all(bf16[16,144,128]{2,1,0:T(8,128)(2,1)S(1)} %bitcast.5), channel_id=1, replica_groups=mesh['blk'=2,'y'=8,'xh'=2,'xl'=2,'tp'=8] {'xl','y'}, dimensions={0} | all-to-all | bytes 1179648 | tf_op jit(solution)/shard_map/all_to_all | solution.py:391
  78.8 1.9 %combine.1 = bf16[128,640]{1,0:T(8,128)(2,1)} custom-call(bf16[2,8,144,128]{3,2,1,0:T(8,128)(2,1)} %bitcast.6), custom_call_target="tpu_custom_call" | custom-call | tf_op jit(solution)/shard_map/combine/pallas_call | solution.py:63
  (2 shorter events, 0.1 us)
Async XLA Ops:
  29.8 15.3 %collective-permute-start = (bf16[8,256,128]{2,1,0:T(8,128)(2,1)S(1)}, bf16[8,256,128]{2,1,0:T(8,128)(2,1)S(1)}, u32[]{:S(2)}, u32[]{:S(2)}) collective-permute-start(bf16[8,256,128]{2,1,0:T(8,128)(2,1)S(1)} %slice.8.own_ref), channel_id=1, source_target_pairs={{0,24},{8,16},{16,8},{24,0},{1,25},{9,17},{17,9},{25,1},{2,26},{10... | collective-permute-start | bytes 1572872 | tf_op jit(solution)/shard_map/ppermute | solution.py:383
  35.8 7.4 %collective-permute-start.1 = (bf16[8,128,128]{2,1,0:T(8,128)(2,1)S(1)}, bf16[8,128,128]{2,1,0:T(8,128)(2,1)S(1)}, u32[]{:S(2)}, u32[]{:S(2)}) collective-permute-start(bf16[8,128,128]{2,1,0:T(8,128)(2,1)S(1)} %slice.9.q_own_ref), channel_id=1, source_target_pairs={{0,8},{8,0},{1,9},{9,1},{2,10},{10,2},{3,11},{11,3},{4,12},{12,4},... | collective-permute-start | bytes 786440 | tf_op jit(solution)/shard_map/ppermute | solution.py:384
  37.8 0.7 copy-start
  38.5 12.6 %collective-permute-start.2 = (bf16[8,256,128]{2,1,0:T(8,128)(2,1)S(1)}, bf16[8,256,128]{2,1,0:T(8,128)(2,1)S(1)}, u32[]{:S(2)}, u32[]{:S(2)}) collective-permute-start(bf16[8,256,128]{2,1,0:T(8,128)(2,1)S(1)} %slice.8.own_ref), channel_id=1, source_target_pairs={{0,256},{1,257},{2,258},{3,259},{4,260},{5,261},{6,262},{7,263},{8... | collective-permute-start | bytes 1572872 | tf_op jit(solution)/shard_map/ppermute | solution.py:385
  45.1 6.2 %collective-permute-start.3 = (bf16[8,256,128]{2,1,0:T(8,128)(2,1)S(1)}, bf16[8,256,128]{2,1,0:T(8,128)(2,1)S(1)}, u32[]{:S(2)}, u32[]{:S(2)}) collective-permute-start(bf16[8,256,128]{2,1,0:T(8,128)(2,1)S(1)} %collective-permute-done.pair_ref), channel_id=1, source_target_pairs={{0,256},{1,257},{2,258},{3,259},{4,260},{5,261},{6,262},{7,263},{8... | collective-permute-start | bytes 1572872 | tf_op jit(solution)/shard_map/ppermute | solution.py:387

commit v5 on v3

--- a/solution.py
+++ b/solution.py
@@ -6,7 +6,7 @@
 from jax import lax
 from jax.experimental import pallas as pl
 from jax.experimental.pallas import tpu as pltpu
-from jax.sharding import Mesh, PartitionSpec as P
+from jax.sharding import PartitionSpec as P
 
 HEAD_DIM = 128
 ROWS = 128
@@ -26,8 +26,11 @@
 NEG = -1e30
 LOG2E = math.log2(math.e)
 C = LOG2E / math.sqrt(HEAD_DIM)
-KEY_PAIRS = [(x, X - 1 - x) for x in range(X)]
-QUERY_PAIRS = [(0, 1), (1, 0)]
+CHIPS = X * Y
+KEY_PAIRS = [(n, n ^ 1) for n in range(CHIPS)]
+QUERY_PAIRS = [(n, n ^ 3) for n in range(CHIPS)]
+COLUMNS = [[y * X + x for y in range(Y)] for x in range(X)]
+COLUMN_PAIRS = [COLUMNS[x] + COLUMNS[X - 1 - x] for x in range(X // 2)]
 
 
 def pack_kernel(q_ref, k_ref, v_ref, out_ref):
@@ -74,7 +77,7 @@
 def places(x, shape):
     n = lax.broadcasted_iota(jnp.int32, shape, 1)
     return (
-        jnp.where(n < 2 * ROWS, x, x ^ 1) * ROWS
+        jnp.where(n < 2 * ROWS, x, X - 1 - x) * ROWS
         + (lax.shift_right_logical(n, 7) & 1) * SPAN
         + (n & (ROWS - 1))
     )
@@ -83,8 +86,8 @@
 def find_documents(blk, x, int_ref, first_ref, lo_ref, hi_ref):
     base = blk * GROUP
     pos = places(x, (8, TILE)) + lax.broadcasted_iota(jnp.int32, (8, TILE), 0) * WIDE
-    lowest = jnp.minimum(x, x ^ 1) * ROWS
-    highest = SPAN + jnp.maximum(x, x ^ 1) * ROWS + ROWS - 1
+    lowest = jnp.minimum(x, X - 1 - x) * ROWS
+    highest = SPAN + jnp.maximum(x, X - 1 - x) * ROWS + ROWS - 1
     start = -base
     first = jnp.zeros((8, TILE), jnp.int32) - base
     los = [start] * TILES
@@ -102,7 +105,7 @@
 
 def key_places(x):
     row = lax.broadcasted_iota(jnp.int32, (HALF, HALF), 0)
-    return jnp.where(row < ROWS, x, X - 1 - x) * ROWS + (row & (ROWS - 1))
+    return jnp.where(row < ROWS, x, x ^ 1) * ROWS + (row & (ROWS - 1))
 
 
 def load_queries(q_own_ref, q_pair_ref, i):
@@ -328,7 +331,7 @@
             stats = stats.astype(jnp.bfloat16)
             for n in range(4):
                 part = slice(n * ROWS, (n + 1) * ROWS)
-                y, to = 2 * i + (n & 1), (x & 1) ^ (n >> 1)
+                y, to = 2 * i + (n & 1), lax.shift_right_logical(x, 1) ^ (n >> 1)
                 o_ref[to, y, :ROWS, :] = o[:, part]
                 o_ref[to, y, ROWS:, :] = stats[:, part]
 
@@ -379,27 +382,26 @@
 
 
 def body(queries, keys, values, lengths):
-    x = 2 * lax.axis_index("xh") + lax.axis_index("xl")
-    place = jnp.stack([lax.axis_index("blk"), x, lax.axis_index("y")]).astype(jnp.int32)
+    chip = lax.axis_index("ctx")
+    place = jnp.stack([lax.axis_index("blk"), chip % X, chip // X]).astype(jnp.int32)
     ints = jnp.concatenate([place, lengths])
-    got = lax.all_to_all(pack(queries, keys, values), "y", 0, 0, tiled=True)
+    packed = pack(queries, keys, values)
+    got = lax.all_to_all(packed, "ctx", 0, 0, tiled=True, axis_index_groups=COLUMNS)
     own_queries, own = got[:, :ROWS], got[:, ROWS:]
-    pair = lax.ppermute(own, ("xh", "xl"), KEY_PAIRS)
-    pair_queries = lax.ppermute(own_queries, "xl", QUERY_PAIRS)
+    pair = lax.ppermute(own, "ctx", KEY_PAIRS)
+    pair_queries = lax.ppermute(own_queries, "ctx", QUERY_PAIRS)
     prev_own = lax.ppermute(own, "blk", [(0, 1)])
     pair, pair_queries, ints = lax.optimization_barrier((pair, pair_queries, ints))
     prev_pair = lax.ppermute(pair, "blk", [(0, 1)])
     state = attend_own(ints, own_queries, pair_queries, own, pair)
     parts = attend_prev(ints, own_queries, pair_queries, prev_own, prev_pair, *state)
     parts = parts.reshape(2 * Y, ROWS + STATS, HEAD_DIM)
-    parts = lax.all_to_all(parts, ("xl", "y"), 0, 0, tiled=True)
+    parts = lax.all_to_all(parts, "ctx", 0, 0, tiled=True, axis_index_groups=COLUMN_PAIRS)
     return combine(parts.reshape(2, Y, ROWS + STATS, HEAD_DIM))
 
 
 def solution(mesh):
-    devices = mesh.devices.reshape(2, Y, 2, 2, mesh.devices.shape[2])
-    fine = Mesh(devices, ("blk", "y", "xh", "xl", "tp"))
-    rows = P(("blk", "y", "xh", "xl"), "tp")
+    rows = P(("blk", "ctx"), "tp")
     return jax.shard_map(
-        body, mesh=fine, in_specs=(rows, rows, rows, P()), out_specs=rows, check_vma=False
+        body, mesh=mesh, in_specs=(rows, rows, rows, P()), out_specs=rows, check_vma=False
     )

time: 79.6 us -> 82.6 us (1.038)
  blocking collectives: 50 us -> 52.5 us
  Pallas kernels: 12.5 us -> 14.5 us
  waiting for transfers between devices: 5.31 us -> 3.44 us
    all_to_all x2, blocking collectives: 50 us -> 52.5 us  [the longest x1 27.6 us: body(): lax.all_to_all(packed, 'ctx', 0, 0, tiled=True, axis_index_groups=COLUMNS)]
    pallas_call x1, Pallas kernels: 3.18 us -> 5.09 us  [attend_prev(): pl.pallas_call(prev_kernel, out_shape=jax.ShapeDtypeStruct((2, Y, ROWS +...]
    ppermute x2, waiting for transfers between devices: 5.31 us -> 3.44 us  [the longest x1 2.55 us: body(): pair_queries = lax.ppermute(own_queries, 'ctx', QUERY_PAIRS)]
where the time goes in v5:
time: 82.6 us; the launch traced here: 82.3 us
  blocking collectives  52.5 us (64%)
  Pallas kernels  14.5 us (18%)
  starting transfers between devices  11.1 us (13%)
  waiting for transfers between devices  3.44 us (4%)
    all_to_all x1, blocking collectives, body(): lax.all_to_all(packed, 'ctx', 0, 0, tiled=True, axis_index_groups=COLUMNS)  27.6 us
    all_to_all x1, blocking collectives, body(): lax.all_to_all(parts, 'ctx', 0, 0, tiled=True, axis_index_groups=COLUMN_P...  24.8 us
    pallas_call x1, Pallas kernels, attend_own(): pl.pallas_call(own_kernel, out_shape=(jax.ShapeDtypeStruct(ACC, jnp.float...  5.44 us
    pallas_call x1, Pallas kernels, attend_prev(): pl.pallas_call(prev_kernel, out_shape=jax.ShapeDtypeStruct((2, Y, ROWS +...  5.09 us
    ppermute x1, starting transfers between devices, body(): pair = lax.ppermute(own, 'ctx', KEY_PAIRS)  4.77 us
    ppermute x1, starting transfers between devices, body(): pair_queries = lax.ppermute(own_queries, 'ctx', QUERY_PAIRS)  3.72 us
    ppermute x1, waiting for transfers between devices, body(): pair_queries = lax.ppermute(own_queries, 'ctx', QUERY_PAIRS)  2.55 us
    pallas_call x1, Pallas kernels, pack(): pl.pallas_call(pack_kernel, out_shape=jax.ShapeDtypeStruct((Y, 2 * ROWS +...  2.11 us
  transfers between devices with their start and end apart: 4, of which 2 were waited for; matrix products, arithmetic and copies ran while one was open for 0% of the time, Pallas kernels for 7%

profile of v5, /device:TPU:1, one launch (start us, length us, event | category | flops | bytes accessed | tf_op | source)
XLA Modules:
  0.0 82.3 jit_solution(6609730772184923300)
XLA Ops:
  0.0 2.1 %pack.1 = bf16[8,384,128]{2,1,0:T(8,128)(2,1)} custom-call(bf16[128,640]{1,0:T(8,128)(2,1)} %q_ref.1, bf16[128,640]{1,0:T(8,128)(2,1)} %k_ref.1, bf16[128,640]{1,0:T(8,128)(2,1)} %v_ref.1), custom_call_target="tpu_custom_call" | custom-call | tf_op jit(solution)/shard_map/pack/pallas_call | solution.py:45
  2.1 27.6 %all_to_all.10 = bf16[8,384,128]{2,1,0:T(8,128)(2,1)S(1)} all-to-all(bf16[8,384,128]{2,1,0:T(8,128)(2,1)} %pack.1), channel_id=1, replica_groups={{0,32,64,96,128,160,192,224},{8,40,72,104,136,168,200,232},{16,48,80,11..., dimensions={0} | all-to-all | bytes 1572864 | tf_op jit(solution)/shard_map/all_to_all | solution.py:389
  29.8 4.8 %collective-permute-start = (bf16[8,256,128]{2,1,0:T(8,128)(2,1)S(1)}, bf16[8,256,128]{2,1,0:T(8,128)(2,1)S(1)}, u32[]{:S(2)}, u32[]{:S(2)}) collective-permute-start(bf16[8,256,128]{2,1,0:T(8,128)(2,1)S(1)} %slice.8.own_ref), channel_id=1, source_target_pairs={{0,8},{8,0},{16,24},{24,16},{32,40},{40,32},{48,56},{56,48},{64,72... | collective-permute-start | bytes 1572872 | tf_op jit(solution)/shard_map/ppermute | solution.py:391
  34.6 3.7 %collective-permute-start.1 = (bf16[8,128,128]{2,1,0:T(8,128)(2,1)S(1)}, bf16[8,128,128]{2,1,0:T(8,128)(2,1)S(1)}, u32[]{:S(2)}, u32[]{:S(2)}) collective-permute-start(bf16[8,128,128]{2,1,0:T(8,128)(2,1)S(1)} %slice.9.q_own_ref), channel_id=1, source_target_pairs={{0,24},{8,16},{16,8},{24,0},{32,56},{40,48},{48,40},{56,32},{64,88... | collective-permute-start | bytes 786440 | tf_op jit(solution)/shard_map/ppermute | solution.py:392
  38.3 0.0 copy-start
  38.3 0.6 copy-done
  39.0 0.1 pad_add_fusion.int_ref
  39.1 1.3 %collective-permute-start.2 = (bf16[8,256,128]{2,1,0:T(8,128)(2,1)S(1)}, bf16[8,256,128]{2,1,0:T(8,128)(2,1)S(1)}, u32[]{:S(2)}, u32[]{:S(2)}) collective-permute-start(bf16[8,256,128]{2,1,0:T(8,128)(2,1)S(1)} %slice.8.own_ref), channel_id=1, source_target_pairs={{0,256},{1,257},{2,258},{3,259},{4,260},{5,261},{6,262},{7,263},{8... | collective-permute-start | bytes 1572872 | tf_op jit(solution)/shard_map/ppermute | solution.py:393
  40.3 2.5 %collective-permute-done.1.q_pair_ref = bf16[8,128,128]{2,1,0:T(8,128)(2,1)S(1)} collective-permute-done((bf16[8,128,128]{2,1,0:T(8,128)(2,1)S(1)}, bf16[8,128,128]{2,1,0:T(8,128)(2,1)S(1)}, u32[]{:S(2)}, u32[]{:S(2)}) %collective-permute-start.1) | collective-permute-done | bytes 262176 | tf_op jit(solution)/shard_map/ppermute | solution.py:392
  42.9 0.9 %collective-permute-done.pair_ref = bf16[8,256,128]{2,1,0:T(8,128)(2,1)S(1)} collective-permute-done((bf16[8,256,128]{2,1,0:T(8,128)(2,1)S(1)}, bf16[8,256,128]{2,1,0:T(8,128)(2,1)S(1)}, u32[]{:S(2)}, u32[]{:S(2)}) %collective-permute-start) | collective-permute-done | bytes 524320 | tf_op jit(solution)/shard_map/ppermute | solution.py:391
  43.8 1.3 %collective-permute-start.3 = (bf16[8,256,128]{2,1,0:T(8,128)(2,1)S(1)}, bf16[8,256,128]{2,1,0:T(8,128)(2,1)S(1)}, u32[]{:S(2)}, u32[]{:S(2)}) collective-permute-start(bf16[8,256,128]{2,1,0:T(8,128)(2,1)S(1)} %collective-permute-done.pair_ref), channel_id=1, source_target_pairs={{0,256},{1,257},{2,258},{3,259},{4,260},{5,261},{6,262},{7,263},{8... | collective-permute-start | bytes 1572872 | tf_op jit(solution)/shard_map/ppermute | solution.py:395
  45.1 5.4 %attend_own.1 = (f32[4,128,512]{2,1,0:T(8,128)S(1)}, f32[4,8,512]{2,1,0:T(8,128)S(1)}) custom-call(s32[35]{0:T(128)S(1)} %pad_add_fusion.int_ref, bf16[8,128,128]{2,1,0:T(8,128)(2,1)S(1)} %slice.9.q_own_ref, bf16[8,128,128]{2,1,0:T(8,128)(2,1)S(1)} %collective-permute-done.1.q_pair_ref, bf16[8,256,128]{2,1,0:T(8,128)(2,1)S(1)} %slice.8.own_ref, ...), custom_call_target="tpu_custom_call" | custom-call | flops 1073741824 | bytes 4194304 | tf_op jit(solution)/shard_map/attend_own/pallas_call | solution.py:352
  50.5 0.0 collective-permute-done.2.prev_own_ref
  50.5 0.0 collective-permute-done.3.prev_pair_ref
  50.5 5.1 %attend_prev.1 = bf16[2,8,144,128]{3,2,1,0:T(8,128)(2,1)S(1)} custom-call(s32[35]{0:T(128)S(1)} %pad_add_fusion.int_ref, bf16[8,128,128]{2,1,0:T(8,128)(2,1)S(1)} %slice.9.q_own_ref, bf16[8,128,128]{2,1,0:T(8,128)(2,1)S(1)} %collective-permute-done.1.q_pair_ref, bf16[8,256,128]{2,1,0:T(8,128)(2,1)S(1)} %collective-permute-done.2.prev_own_ref, ...), custom_call_target="tpu_custom_call" | custom-call | flops 536870912 | bytes 4194304 | tf_op jit(solution)/shard_map/attend_prev/pallas_call | solution.py:370
  55.6 24.8 %all_to_all.11 = bf16[16,144,128]{2,1,0:T(8,128)(2,1)} all-to-all(bf16[16,144,128]{2,1,0:T(8,128)(2,1)S(1)} %bitcast.5), channel_id=1, replica_groups={{0,32,64,96,128,160,192,224,24,56,88,120,152,184,216,248},{8,40,72,104,..., dimensions={0} | all-to-all | bytes 1179648 | tf_op jit(solution)/shard_map/all_to_all | solution.py:399
  80.5 1.8 %combine.1 = bf16[128,640]{1,0:T(8,128)(2,1)} custom-call(bf16[2,8,144,128]{3,2,1,0:T(8,128)(2,1)} %bitcast.6), custom_call_target="tpu_custom_call" | custom-call | tf_op jit(solution)/shard_map/combine/pallas_call | solution.py:67
  (2 shorter events, 0.1 us)
Async XLA Ops:
  29.8 14.0 %collective-permute-start = (bf16[8,256,128]{2,1,0:T(8,128)(2,1)S(1)}, bf16[8,256,128]{2,1,0:T(8,128)(2,1)S(1)}, u32[]{:S(2)}, u32[]{:S(2)}) collective-permute-start(bf16[8,256,128]{2,1,0:T(8,128)(2,1)S(1)} %slice.8.own_ref), channel_id=1, source_target_pairs={{0,8},{8,0},{16,24},{24,16},{32,40},{40,32},{48,56},{56,48},{64,72... | collective-permute-start | bytes 1572872 | tf_op jit(solution)/shard_map/ppermute | solution.py:391
  34.6 8.3 %collective-permute-start.1 = (bf16[8,128,128]{2,1,0:T(8,128)(2,1)S(1)}, bf16[8,128,128]{2,1,0:T(8,128)(2,1)S(1)}, u32[]{:S(2)}, u32[]{:S(2)}) collective-permute-start(bf16[8,128,128]{2,1,0:T(8,128)(2,1)S(1)} %slice.9.q_own_ref), channel_id=1, source_target_pairs={{0,24},{8,16},{16,8},{24,0},{32,56},{40,48},{48,40},{56,32},{64,88... | collective-permute-start | bytes 786440 | tf_op jit(solution)/shard_map/ppermute | solution.py:392
  38.3 0.7 copy-start
  39.1 11.5 %collective-permute-start.2 = (bf16[8,256,128]{2,1,0:T(8,128)(2,1)S(1)}, bf16[8,256,128]{2,1,0:T(8,128)(2,1)S(1)}, u32[]{:S(2)}, u32[]{:S(2)}) collective-permute-start(bf16[8,256,128]{2,1,0:T(8,128)(2,1)S(1)} %slice.8.own_ref), channel_id=1, source_target_pairs={{0,256},{1,257},{2,258},{3,259},{4,260},{5,261},{6,262},{7,263},{8... | collective-permute-start | bytes 1572872 | tf_op jit(solution)/shard_map/ppermute | solution.py:393
  43.8 6.7 %collective-permute-start.3 = (bf16[8,256,128]{2,1,0:T(8,128)(2,1)S(1)}, bf16[8,256,128]{2,1,0:T(8,128)(2,1)S(1)}, u32[]{:S(2)}, u32[]{:S(2)}) collective-permute-start(bf16[8,256,128]{2,1,0:T(8,128)(2,1)S(1)} %collective-permute-done.pair_ref), channel_id=1, source_target_pairs={{0,256},{1,257},{2,258},{3,259},{4,260},{5,261},{6,262},{7,263},{8... | collective-permute-start | bytes 1572872 | tf_op jit(solution)/shard_map/ppermute | solution.py:395

commit v6 on v5

--- a/solution.py
+++ b/solution.py
@@ -6,7 +6,7 @@
 from jax import lax
 from jax.experimental import pallas as pl
 from jax.experimental.pallas import tpu as pltpu
-from jax.sharding import PartitionSpec as P
+from jax.sharding import Mesh, PartitionSpec as P
 
 HEAD_DIM = 128
 ROWS = 128
@@ -22,15 +22,17 @@
 TILES = Y // 2
 GROUP = Y * SPAN
 STATS = 16
-PLACE = 3
+PLACE = 6
 NEG = -1e30
 LOG2E = math.log2(math.e)
 C = LOG2E / math.sqrt(HEAD_DIM)
 CHIPS = X * Y
-KEY_PAIRS = [(n, n ^ 1) for n in range(CHIPS)]
-QUERY_PAIRS = [(n, n ^ 3) for n in range(CHIPS)]
-COLUMNS = [[y * X + x for y in range(Y)] for x in range(X)]
-COLUMN_PAIRS = [COLUMNS[x] + COLUMNS[X - 1 - x] for x in range(X // 2)]
+KEY_PAIRS = [(n, n ^ (1 if n >= CHIPS else 3)) for n in range(2 * CHIPS)]
+QUERY_PAIRS = [(n, n ^ (3 if n >= CHIPS else 1)) for n in range(2 * CHIPS)]
+PREV_OWN = [(n, CHIPS + n) for n in range(CHIPS)]
+PREV_PAIR = [(n, CHIPS + (n ^ 1)) for n in range(CHIPS)]
+COLUMNS = [[g * CHIPS + y * X + x for y in range(Y)] for g in range(2) for x in range(X)]
+COLUMN_PAIRS = [COLUMNS[a] + COLUMNS[b] for a, b in ((0, 1), (2, 3), (4, 7), (5, 6))]
 
 
 def pack_kernel(q_ref, k_ref, v_ref, out_ref):
@@ -74,20 +76,21 @@
     )(parts)
 
 
-def places(x, shape):
+def places(x, pair_x, shape):
     n = lax.broadcasted_iota(jnp.int32, shape, 1)
     return (
-        jnp.where(n < 2 * ROWS, x, X - 1 - x) * ROWS
+        jnp.where(n < 2 * ROWS, x, pair_x) * ROWS
         + (lax.shift_right_logical(n, 7) & 1) * SPAN
         + (n & (ROWS - 1))
     )
 
 
-def find_documents(blk, x, int_ref, first_ref, lo_ref, hi_ref):
-    base = blk * GROUP
-    pos = places(x, (8, TILE)) + lax.broadcasted_iota(jnp.int32, (8, TILE), 0) * WIDE
-    lowest = jnp.minimum(x, X - 1 - x) * ROWS
-    highest = SPAN + jnp.maximum(x, X - 1 - x) * ROWS + ROWS - 1
+def find_documents(int_ref, first_ref, lo_ref, hi_ref):
+    x, pair_x = int_ref[1], int_ref[3]
+    base = int_ref[0] * GROUP
+    pos = places(x, pair_x, (8, TILE)) + lax.broadcasted_iota(jnp.int32, (8, TILE), 0) * WIDE
+    lowest = jnp.minimum(x, pair_x) * ROWS
+    highest = SPAN + jnp.maximum(x, pair_x) * ROWS + ROWS - 1
     start = -base
     first = jnp.zeros((8, TILE), jnp.int32) - base
     los = [start] * TILES
@@ -103,9 +106,9 @@
         hi_ref[i] = lax.shift_right_arithmetic(his[i], WIDE_SHIFT)
 
 
-def key_places(x):
+def key_places(x, pair_x):
     row = lax.broadcasted_iota(jnp.int32, (HALF, HALF), 0)
-    return jnp.where(row < ROWS, x, x ^ 1) * ROWS + (row & (ROWS - 1))
+    return jnp.where(row < ROWS, x, pair_x) * ROWS + (row & (ROWS - 1))
 
 
 def load_queries(q_own_ref, q_pair_ref, i):
@@ -179,17 +182,17 @@
 
     @pl.when(slot < HEADS)
     def _():
-        find_documents(blk, x, int_ref, first_ref, lo_ref, hi_ref)
+        find_documents(int_ref, first_ref, lo_ref, hi_ref)
 
         refs = (own_ref, pair_ref)
-        key_rows = key_places(x)
+        key_rows = key_places(x, int_ref[4])
 
         def score(s_ref, i, q, g, masked, diagonal, n, c, m):
             kept = None
             if masked:
                 kept = key_rows >= first_ref[i : i + 1, piece(c)] - (g * WIDE + n * SPAN)
                 if diagonal:
-                    kept &= key_rows <= places(x, (1, TILE))[:, piece(c)] - n * SPAN
+                    kept &= key_rows <= places(x, int_ref[3], (1, TILE))[:, piece(c)] - n * SPAN
             return scores_of(refs, s_ref, q, g, n, m, kept, c)
 
         def score_diagonal(s_ref, i, q, m):
@@ -258,13 +261,13 @@
     def _():
         @pl.when(blk > 0)
         def _():
-            find_documents(blk, x, int_ref, first_ref, lo_ref, hi_ref)
+            find_documents(int_ref, first_ref, lo_ref, hi_ref)
 
         def begin_of(i):
             return jnp.where(blk > 0, jnp.clip(lo_ref[i] + TILES, 0, TILES), TILES)
 
         refs = (prev_own_ref, prev_pair_ref)
-        key_rows = key_places(x)
+        key_rows = key_places(x, int_ref[4])
 
         def score(s_ref, i, q, g, masked, n, c, m):
             kept = None
@@ -331,7 +334,7 @@
             stats = stats.astype(jnp.bfloat16)
             for n in range(4):
                 part = slice(n * ROWS, (n + 1) * ROWS)
-                y, to = 2 * i + (n & 1), lax.shift_right_logical(x, 1) ^ (n >> 1)
+                y, to = 2 * i + (n & 1), int_ref[5] ^ (n >> 1)
                 o_ref[to, y, :ROWS, :] = o[:, part]
                 o_ref[to, y, ROWS:, :] = stats[:, part]
 
@@ -382,26 +385,34 @@
 
 
 def body(queries, keys, values, lengths):
-    chip = lax.axis_index("ctx")
-    place = jnp.stack([lax.axis_index("blk"), chip % X, chip // X]).astype(jnp.int32)
+    chip = lax.axis_index("tokens")
+    blk, x, y = chip // CHIPS, chip % X, chip // X % Y
+    first = blk == 0
+    pairs = [jnp.where(first, x ^ 1, x ^ 3), jnp.where(first, x ^ 3, x ^ 1)]
+    place = jnp.stack([blk, x, y, *pairs, jnp.where(first, x & 1, x // 2)]).astype(jnp.int32)
     ints = jnp.concatenate([place, lengths])
     packed = pack(queries, keys, values)
-    got = lax.all_to_all(packed, "ctx", 0, 0, tiled=True, axis_index_groups=COLUMNS)
+    got = lax.all_to_all(packed, "tokens", 0, 0, tiled=True, axis_index_groups=COLUMNS)
     own_queries, own = got[:, :ROWS], got[:, ROWS:]
-    pair = lax.ppermute(own, "ctx", KEY_PAIRS)
-    pair_queries = lax.ppermute(own_queries, "ctx", QUERY_PAIRS)
-    prev_own = lax.ppermute(own, "blk", [(0, 1)])
-    pair, pair_queries, ints = lax.optimization_barrier((pair, pair_queries, ints))
-    prev_pair = lax.ppermute(pair, "blk", [(0, 1)])
+    pair = lax.ppermute(own, "tokens", KEY_PAIRS)
+    pair_queries = lax.ppermute(own_queries, "tokens", QUERY_PAIRS)
+    prev_own = lax.ppermute(own, "tokens", PREV_OWN)
+    later, pair_queries, ints = lax.optimization_barrier((own, pair_queries, ints))
+    prev_pair = lax.ppermute(later, "tokens", PREV_PAIR)
     state = attend_own(ints, own_queries, pair_queries, own, pair)
     parts = attend_prev(ints, own_queries, pair_queries, prev_own, prev_pair, *state)
     parts = parts.reshape(2 * Y, ROWS + STATS, HEAD_DIM)
-    parts = lax.all_to_all(parts, "ctx", 0, 0, tiled=True, axis_index_groups=COLUMN_PAIRS)
+    parts = lax.all_to_all(parts, "tokens", 0, 0, tiled=True, axis_index_groups=COLUMN_PAIRS)
     return combine(parts.reshape(2, Y, ROWS + STATS, HEAD_DIM))
 
 
 def solution(mesh):
-    rows = P(("blk", "ctx"), "tp")
+    devices = mesh.devices.reshape(2 * CHIPS, mesh.devices.shape[2])
+    rows = P("tokens", "tp")
     return jax.shard_map(
-        body, mesh=mesh, in_specs=(rows, rows, rows, P()), out_specs=rows, check_vma=False
+        body,
+        mesh=Mesh(devices, ("tokens", "tp")),
+        in_specs=(rows, rows, rows, P()),
+        out_specs=rows,
+        check_vma=False,
     )

time: 82.6 us -> 81 us (0.981)
  blocking collectives: 52.5 us -> 47.4 us
  waiting for transfers between devices: 3.44 us -> 8.32 us
    all_to_all x2, blocking collectives: 52.5 us -> 47.4 us  [the longest x1 27.6 us: body(): lax.all_to_all(packed, 'tokens', 0, 0, tiled=True, axis_index_groups=COLU...]
    ppermute x4, waiting for transfers between devices: 3.44 us -> 8.32 us  [the longest x1 6.16 us: body(): pair = lax.ppermute(own, 'tokens', KEY_PAIRS)]
    pallas_call x1, Pallas kernels: 5.44 us -> 4.31 us  [attend_own(): pl.pallas_call(own_kernel, out_shape=(jax.ShapeDtypeStruct(ACC, jnp.float...]
  transfers between devices with their start and end apart: 4 -> 4, of which waited for: 2 -> 2; matrix products, arithmetic and copies ran while one was open for 0% -> 0% of each run, Pallas kernels for 7% -> 5%
where the time goes in v6:
time: 81 us
  blocking collectives  47.4 us (59%)
  Pallas kernels  13.9 us (17%)
  starting transfers between devices  10.5 us (13%)
  waiting for transfers between devices  8.32 us (10%)
    all_to_all x1, blocking collectives, body(): lax.all_to_all(packed, 'tokens', 0, 0, tiled=True, axis_index_groups=COLU...  27.6 us
    all_to_all x1, blocking collectives, body(): lax.all_to_all(parts, 'tokens', 0, 0, tiled=True, axis_index_groups=COLUM...  19.8 us
    ppermute x1, waiting for transfers between devices, body(): pair = lax.ppermute(own, 'tokens', KEY_PAIRS)  6.16 us
    ppermute x1, starting transfers between devices, body(): pair_queries = lax.ppermute(own_queries, 'tokens', QUERY_PAIRS)  6.03 us
    pallas_call x1, Pallas kernels, attend_prev(): pl.pallas_call(prev_kernel, out_shape=jax.ShapeDtypeStruct((2, Y, ROWS +...  5.64 us
    pallas_call x1, Pallas kernels, attend_own(): pl.pallas_call(own_kernel, out_shape=(jax.ShapeDtypeStruct(ACC, jnp.float...  4.31 us
    ppermute x1, waiting for transfers between devices, body(): prev_pair = lax.ppermute(later, 'tokens', PREV_PAIR)  2.16 us
    pallas_call x1, Pallas kernels, pack(): pl.pallas_call(pack_kernel, out_shape=jax.ShapeDtypeStruct((Y, 2 * ROWS +...  2.11 us
  transfers between devices with their start and end apart: 4, of which 2 were waited for; matrix products, arithmetic and copies ran while one was open for 0% of the time, Pallas kernels for 5%

profile of v6, /device:TPU:1, one launch (start us, length us, event | category | flops | bytes accessed | tf_op | source)
XLA Modules:
  0.0 81.0 jit_solution(2031023516588983348)
XLA Ops:
  0.0 2.1 %pack.1 = bf16[8,384,128]{2,1,0:T(8,128)(2,1)} custom-call(bf16[128,640]{1,0:T(8,128)(2,1)} %q_ref.1, bf16[128,640]{1,0:T(8,128)(2,1)} %k_ref.1, bf16[128,640]{1,0:T(8,128)(2,1)} %v_ref.1), custom_call_target="tpu_custom_call" | custom-call | tf_op jit(solution)/shard_map/pack/pallas_call | solution.py:47
  2.1 27.6 %all_to_all.10 = bf16[8,384,128]{2,1,0:T(8,128)(2,1)S(1)} all-to-all(bf16[8,384,128]{2,1,0:T(8,128)(2,1)} %pack.1), channel_id=1, replica_groups={{0,32,64,96,128,160,192,224},{8,40,72,104,136,168,200,232},{16,48,80,11..., dimensions={0} | all-to-all | bytes 1572864 | tf_op jit(solution)/shard_map/all_to_all | solution.py:395
  29.7 6.0 %collective-permute-start = (bf16[8,128,128]{2,1,0:T(8,128)(2,1)S(1)}, bf16[8,128,128]{2,1,0:T(8,128)(2,1)S(1)}, u32[]{:S(2)}, u32[]{:S(2)}) collective-permute-start(bf16[8,128,128]{2,1,0:T(8,128)(2,1)S(1)} %slice.9.q_own_ref), channel_id=1, source_target_pairs={{0,8},{8,0},{16,24},{24,16},{32,40},{40,32},{48,56},{56,48},{64,72... | collective-permute-start | bytes 786440 | tf_op jit(solution)/shard_map/ppermute | solution.py:398
  35.8 1.9 %collective-permute-start.3 = (bf16[8,256,128]{2,1,0:T(8,128)(2,1)S(1)}, bf16[8,256,128]{2,1,0:T(8,128)(2,1)S(1)}, u32[]{:S(2)}, u32[]{:S(2)}) collective-permute-start(bf16[8,256,128]{2,1,0:T(8,128)(2,1)S(1)} %slice.8.own_ref), channel_id=1, source_target_pairs={{0,24},{8,16},{16,8},{24,0},{32,56},{40,48},{48,40},{56,32},{64,88... | collective-permute-start | bytes 1572872 | tf_op jit(solution)/shard_map/ppermute | solution.py:397
  37.8 0.0 copy-start
  37.8 0.6 copy-done
  38.5 0.1 concatenate.3.int_ref
  38.6 1.3 %collective-permute-start.1 = (bf16[8,256,128]{2,1,0:T(8,128)(2,1)S(1)}, bf16[8,256,128]{2,1,0:T(8,128)(2,1)S(1)}, u32[]{:S(2)}, u32[]{:S(2)}) collective-permute-start(bf16[8,256,128]{2,1,0:T(8,128)(2,1)S(1)} %slice.8.own_ref), channel_id=1, source_target_pairs={{0,256},{8,264},{16,272},{24,280},{32,288},{40,296},{48,304},{56,3... | collective-permute-start | bytes 1572872 | tf_op jit(solution)/shard_map/ppermute | solution.py:399
  39.9 0.0 collective-permute-done.q_pair_ref
  39.9 1.3 %collective-permute-start.2 = (bf16[8,256,128]{2,1,0:T(8,128)(2,1)S(1)}, bf16[8,256,128]{2,1,0:T(8,128)(2,1)S(1)}, u32[]{:S(2)}, u32[]{:S(2)}) collective-permute-start(bf16[8,256,128]{2,1,0:T(8,128)(2,1)S(1)} %slice.8.own_ref), channel_id=1, source_target_pairs={{0,264},{8,256},{16,280},{24,272},{32,296},{40,288},{48,312},{56,3... | collective-permute-start | bytes 1572872 | tf_op jit(solution)/shard_map/ppermute | solution.py:401
  41.2 6.2 %collective-permute-done.3.pair_ref = bf16[8,256,128]{2,1,0:T(8,128)(2,1)S(1)} collective-permute-done((bf16[8,256,128]{2,1,0:T(8,128)(2,1)S(1)}, bf16[8,256,128]{2,1,0:T(8,128)(2,1)S(1)}, u32[]{:S(2)}, u32[]{:S(2)}) %collective-permute-start.3) | collective-permute-done | bytes 524320 | tf_op jit(solution)/shard_map/ppermute | solution.py:397
  47.3 4.3 %attend_own.1 = (f32[4,128,512]{2,1,0:T(8,128)S(1)}, f32[4,8,512]{2,1,0:T(8,128)S(1)}) custom-call(s32[38]{0:T(128)S(1)} %concatenate.3.int_ref, bf16[8,128,128]{2,1,0:T(8,128)(2,1)S(1)} %slice.9.q_own_ref, bf16[8,128,128]{2,1,0:T(8,128)(2,1)S(1)} %collective-permute-done.q_pair_ref, bf16[8,256,128]{2,1,0:T(8,128)(2,1)S(1)} %slice.8.own_ref, ...), custom_call_target="tpu_custom_call" | custom-call | flops 1073741824 | bytes 4194304 | tf_op jit(solution)/shard_map/attend_own/pallas_call | solution.py:355
  51.6 0.0 collective-permute-done.1.prev_own_ref
  51.7 2.2 %collective-permute-done.2.prev_pair_ref = bf16[8,256,128]{2,1,0:T(8,128)(2,1)S(1)} collective-permute-done((bf16[8,256,128]{2,1,0:T(8,128)(2,1)S(1)}, bf16[8,256,128]{2,1,0:T(8,128)(2,1)S(1)}, u32[]{:S(2)}, u32[]{:S(2)}) %collective-permute-start.2) | collective-permute-done | bytes 524320 | tf_op jit(solution)/shard_map/ppermute | solution.py:401
  53.8 5.6 %attend_prev.1 = bf16[2,8,144,128]{3,2,1,0:T(8,128)(2,1)S(1)} custom-call(s32[38]{0:T(128)S(1)} %concatenate.3.int_ref, bf16[8,128,128]{2,1,0:T(8,128)(2,1)S(1)} %slice.9.q_own_ref, bf16[8,128,128]{2,1,0:T(8,128)(2,1)S(1)} %collective-permute-done.q_pair_ref, bf16[8,256,128]{2,1,0:T(8,128)(2,1)S(1)} %collective-permute-done.1.prev_own_ref, ...), custom_call_target="tpu_custom_call" | custom-call | flops 536870912 | bytes 4194304 | tf_op jit(solution)/shard_map/attend_prev/pallas_call | solution.py:373
  59.5 19.8 %all_to_all.11 = bf16[16,144,128]{2,1,0:T(8,128)(2,1)} all-to-all(bf16[16,144,128]{2,1,0:T(8,128)(2,1)S(1)} %bitcast.8), channel_id=1, replica_groups={{0,32,64,96,128,160,192,224,8,40,72,104,136,168,200,232},{16,48,80,112,..., dimensions={0} | all-to-all | bytes 1179648 | tf_op jit(solution)/shard_map/all_to_all | solution.py:405
  79.2 1.8 %combine.1 = bf16[128,640]{1,0:T(8,128)(2,1)} custom-call(bf16[2,8,144,128]{3,2,1,0:T(8,128)(2,1)} %bitcast.9), custom_call_target="tpu_custom_call" | custom-call | tf_op jit(solution)/shard_map/combine/pallas_call | solution.py:69
  (2 shorter events, 0.1 us)
Async XLA Ops:
  29.7 10.1 %collective-permute-start = (bf16[8,128,128]{2,1,0:T(8,128)(2,1)S(1)}, bf16[8,128,128]{2,1,0:T(8,128)(2,1)S(1)}, u32[]{:S(2)}, u32[]{:S(2)}) collective-permute-start(bf16[8,128,128]{2,1,0:T(8,128)(2,1)S(1)} %slice.9.q_own_ref), channel_id=1, source_target_pairs={{0,8},{8,0},{16,24},{24,16},{32,40},{40,32},{48,56},{56,48},{64,72... | collective-permute-start | bytes 786440 | tf_op jit(solution)/shard_map/ppermute | solution.py:398
  35.8 11.5 %collective-permute-start.3 = (bf16[8,256,128]{2,1,0:T(8,128)(2,1)S(1)}, bf16[8,256,128]{2,1,0:T(8,128)(2,1)S(1)}, u32[]{:S(2)}, u32[]{:S(2)}) collective-permute-start(bf16[8,256,128]{2,1,0:T(8,128)(2,1)S(1)} %slice.8.own_ref), channel_id=1, source_target_pairs={{0,24},{8,16},{16,8},{24,0},{32,56},{40,48},{48,40},{56,32},{64,88... | collective-permute-start | bytes 1572872 | tf_op jit(solution)/shard_map/ppermute | solution.py:397
  37.8 0.7 copy-start
  38.6 13.1 %collective-permute-start.1 = (bf16[8,256,128]{2,1,0:T(8,128)(2,1)S(1)}, bf16[8,256,128]{2,1,0:T(8,128)(2,1)S(1)}, u32[]{:S(2)}, u32[]{:S(2)}) collective-permute-start(bf16[8,256,128]{2,1,0:T(8,128)(2,1)S(1)} %slice.8.own_ref), channel_id=1, source_target_pairs={{0,256},{8,264},{16,272},{24,280},{32,288},{40,296},{48,304},{56,3... | collective-permute-start | bytes 1572872 | tf_op jit(solution)/shard_map/ppermute | solution.py:399
  39.9 13.9 %collective-permute-start.2 = (bf16[8,256,128]{2,1,0:T(8,128)(2,1)S(1)}, bf16[8,256,128]{2,1,0:T(8,128)(2,1)S(1)}, u32[]{:S(2)}, u32[]{:S(2)}) collective-permute-start(bf16[8,256,128]{2,1,0:T(8,128)(2,1)S(1)} %slice.8.own_ref), channel_id=1, source_target_pairs={{0,264},{8,256},{16,280},{24,272},{32,296},{40,288},{48,312},{56,3... | collective-permute-start | bytes 1572872 | tf_op jit(solution)/shard_map/ppermute | solution.py:401

commit v7 on v6

--- a/solution.py
+++ b/solution.py
@@ -397,7 +397,7 @@
     pair = lax.ppermute(own, "tokens", KEY_PAIRS)
     pair_queries = lax.ppermute(own_queries, "tokens", QUERY_PAIRS)
     prev_own = lax.ppermute(own, "tokens", PREV_OWN)
-    later, pair_queries, ints = lax.optimization_barrier((own, pair_queries, ints))
+    later, pair, pair_queries, ints = lax.optimization_barrier((own, pair, pair_queries, ints))
     prev_pair = lax.ppermute(later, "tokens", PREV_PAIR)
     state = attend_own(ints, own_queries, pair_queries, own, pair)
     parts = attend_prev(ints, own_queries, pair_queries, prev_own, prev_pair, *state)

time: 81 us -> 83.9 us (1.036)
  waiting for transfers between devices: 8.32 us -> 9.56 us
    ppermute x1, waiting for transfers between devices: 6.16 us -> 0.01 us  [body(): pair = lax.ppermute(own, 'tokens', KEY_PAIRS)]
    ppermute x1, waiting for transfers between devices: 0.01 us -> 5.59 us  [body(): pair_queries = lax.ppermute(own_queries, 'tokens', QUERY_PAIRS)]
    ppermute x1, starting transfers between devices: 1.92 us -> 4.77 us  [body(): pair = lax.ppermute(own, 'tokens', KEY_PAIRS)]
    ppermute x1, starting transfers between devices: 6.03 us -> 3.72 us  [body(): pair_queries = lax.ppermute(own_queries, 'tokens', QUERY_PAIRS)]
    ppermute x1, waiting for transfers between devices: 2.16 us -> 3.96 us  [body(): prev_pair = lax.ppermute(later, 'tokens', PREV_PAIR)]
    pallas_call x1, Pallas kernels: 4.31 us -> 5.41 us  [attend_own(): pl.pallas_call(own_kernel, out_shape=(jax.ShapeDtypeStruct(ACC, jnp.float...]
  transfers between devices with their start and end apart: 4 -> 4, of which waited for: 2 -> 2; matrix products, arithmetic and copies ran while one was open for 0% -> 0% of each run, Pallas kernels for 5% -> 6%
where the time goes in v7:
time: 83.9 us; the launch traced here: 83.5 us
  blocking collectives  47.6 us (57%)
  Pallas kernels  14.4 us (17%)
  starting transfers between devices  11.1 us (13%)
  waiting for transfers between devices  9.56 us (11%)
    all_to_all x1, blocking collectives, body(): lax.all_to_all(packed, 'tokens', 0, 0, tiled=True, axis_index_groups=COLU...  27.6 us
    all_to_all x1, blocking collectives, body(): lax.all_to_all(parts, 'tokens', 0, 0, tiled=True, axis_index_groups=COLUM...  20 us
    ppermute x1, waiting for transfers between devices, body(): pair_queries = lax.ppermute(own_queries, 'tokens', QUERY_PAIRS)  5.59 us
    pallas_call x1, Pallas kernels, attend_own(): pl.pallas_call(own_kernel, out_shape=(jax.ShapeDtypeStruct(ACC, jnp.float...  5.41 us
    pallas_call x1, Pallas kernels, attend_prev(): pl.pallas_call(prev_kernel, out_shape=jax.ShapeDtypeStruct((2, Y, ROWS +...  5.06 us
    ppermute x1, starting transfers between devices, body(): pair = lax.ppermute(own, 'tokens', KEY_PAIRS)  4.77 us
    ppermute x1, waiting for transfers between devices, body(): prev_pair = lax.ppermute(later, 'tokens', PREV_PAIR)  3.96 us
    ppermute x1, starting transfers between devices, body(): pair_queries = lax.ppermute(own_queries, 'tokens', QUERY_PAIRS)  3.72 us
  transfers between devices with their start and end apart: 4, of which 2 were waited for; matrix products, arithmetic and copies ran while one was open for 0% of the time, Pallas kernels for 6%

profile of v7, /device:TPU:1, one launch (start us, length us, event | category | flops | bytes accessed | tf_op | source)
XLA Modules:
  0.0 83.5 jit_solution(10333570352376909732)
XLA Ops:
  0.0 2.1 %pack.1 = bf16[8,384,128]{2,1,0:T(8,128)(2,1)} custom-call(bf16[128,640]{1,0:T(8,128)(2,1)} %q_ref.1, bf16[128,640]{1,0:T(8,128)(2,1)} %k_ref.1, bf16[128,640]{1,0:T(8,128)(2,1)} %v_ref.1), custom_call_target="tpu_custom_call" | custom-call | tf_op jit(solution)/shard_map/pack/pallas_call | solution.py:47
  2.1 27.6 %all_to_all.10 = bf16[8,384,128]{2,1,0:T(8,128)(2,1)S(1)} all-to-all(bf16[8,384,128]{2,1,0:T(8,128)(2,1)} %pack.1), channel_id=1, replica_groups={{0,32,64,96,128,160,192,224},{8,40,72,104,136,168,200,232},{16,48,80,11..., dimensions={0} | all-to-all | bytes 1572864 | tf_op jit(solution)/shard_map/all_to_all | solution.py:395
  29.8 4.8 %collective-permute-start = (bf16[8,256,128]{2,1,0:T(8,128)(2,1)S(1)}, bf16[8,256,128]{2,1,0:T(8,128)(2,1)S(1)}, u32[]{:S(2)}, u32[]{:S(2)}) collective-permute-start(bf16[8,256,128]{2,1,0:T(8,128)(2,1)S(1)} %slice.8.own_ref), channel_id=1, source_target_pairs={{0,24},{8,16},{16,8},{24,0},{32,56},{40,48},{48,40},{56,32},{64,88... | collective-permute-start | bytes 1572872 | tf_op jit(solution)/shard_map/ppermute | solution.py:397
  34.6 3.7 %collective-permute-start.1 = (bf16[8,128,128]{2,1,0:T(8,128)(2,1)S(1)}, bf16[8,128,128]{2,1,0:T(8,128)(2,1)S(1)}, u32[]{:S(2)}, u32[]{:S(2)}) collective-permute-start(bf16[8,128,128]{2,1,0:T(8,128)(2,1)S(1)} %slice.9.q_own_ref), channel_id=1, source_target_pairs={{0,8},{8,0},{16,24},{24,16},{32,40},{40,32},{48,56},{56,48},{64,72... | collective-permute-start | bytes 786440 | tf_op jit(solution)/shard_map/ppermute | solution.py:398
  38.4 0.0 copy-start
  38.4 0.6 copy-done
  39.0 0.1 concatenate.3.int_ref
  39.1 1.3 %collective-permute-start.2 = (bf16[8,256,128]{2,1,0:T(8,128)(2,1)S(1)}, bf16[8,256,128]{2,1,0:T(8,128)(2,1)S(1)}, u32[]{:S(2)}, u32[]{:S(2)}) collective-permute-start(bf16[8,256,128]{2,1,0:T(8,128)(2,1)S(1)} %slice.8.own_ref), channel_id=1, source_target_pairs={{0,256},{8,264},{16,272},{24,280},{32,288},{40,296},{48,304},{56,3... | collective-permute-start | bytes 1572872 | tf_op jit(solution)/shard_map/ppermute | solution.py:399
  40.4 5.6 %collective-permute-done.1.q_pair_ref = bf16[8,128,128]{2,1,0:T(8,128)(2,1)S(1)} collective-permute-done((bf16[8,128,128]{2,1,0:T(8,128)(2,1)S(1)}, bf16[8,128,128]{2,1,0:T(8,128)(2,1)S(1)}, u32[]{:S(2)}, u32[]{:S(2)}) %collective-permute-start.1) | collective-permute-done | bytes 262176 | tf_op jit(solution)/shard_map/ppermute | solution.py:398
  46.0 0.0 collective-permute-done.pair_ref
  46.0 1.3 %collective-permute-start.3 = (bf16[8,256,128]{2,1,0:T(8,128)(2,1)S(1)}, bf16[8,256,128]{2,1,0:T(8,128)(2,1)S(1)}, u32[]{:S(2)}, u32[]{:S(2)}) collective-permute-start(bf16[8,256,128]{2,1,0:T(8,128)(2,1)S(1)} %slice.8.own_ref), channel_id=1, source_target_pairs={{0,264},{8,256},{16,280},{24,272},{32,296},{40,288},{48,312},{56,3... | collective-permute-start | bytes 1572872 | tf_op jit(solution)/shard_map/ppermute | solution.py:401
  47.3 5.4 %attend_own.1 = (f32[4,128,512]{2,1,0:T(8,128)S(1)}, f32[4,8,512]{2,1,0:T(8,128)S(1)}) custom-call(s32[38]{0:T(128)S(1)} %concatenate.3.int_ref, bf16[8,128,128]{2,1,0:T(8,128)(2,1)S(1)} %slice.9.q_own_ref, bf16[8,128,128]{2,1,0:T(8,128)(2,1)S(1)} %collective-permute-done.1.q_pair_ref, bf16[8,256,128]{2,1,0:T(8,128)(2,1)S(1)} %slice.8.own_ref, ...), custom_call_target="tpu_custom_call" | custom-call | flops 1073741824 | bytes 4194304 | tf_op jit(solution)/shard_map/attend_own/pallas_call | solution.py:355
  52.7 0.0 collective-permute-done.2.prev_own_ref
  52.7 4.0 %collective-permute-done.3.prev_pair_ref = bf16[8,256,128]{2,1,0:T(8,128)(2,1)S(1)} collective-permute-done((bf16[8,256,128]{2,1,0:T(8,128)(2,1)S(1)}, bf16[8,256,128]{2,1,0:T(8,128)(2,1)S(1)}, u32[]{:S(2)}, u32[]{:S(2)}) %collective-permute-start.3) | collective-permute-done | bytes 524320 | tf_op jit(solution)/shard_map/ppermute | solution.py:401
  56.7 5.1 %attend_prev.1 = bf16[2,8,144,128]{3,2,1,0:T(8,128)(2,1)S(1)} custom-call(s32[38]{0:T(128)S(1)} %concatenate.3.int_ref, bf16[8,128,128]{2,1,0:T(8,128)(2,1)S(1)} %slice.9.q_own_ref, bf16[8,128,128]{2,1,0:T(8,128)(2,1)S(1)} %collective-permute-done.1.q_pair_ref, bf16[8,256,128]{2,1,0:T(8,128)(2,1)S(1)} %collective-permute-done.2.prev_own_ref, ...), custom_call_target="tpu_custom_call" | custom-call | flops 536870912 | bytes 4194304 | tf_op jit(solution)/shard_map/attend_prev/pallas_call | solution.py:373
  61.7 20.0 %all_to_all.11 = bf16[16,144,128]{2,1,0:T(8,128)(2,1)} all-to-all(bf16[16,144,128]{2,1,0:T(8,128)(2,1)S(1)} %bitcast.8), channel_id=1, replica_groups={{0,32,64,96,128,160,192,224,8,40,72,104,136,168,200,232},{16,48,80,112,..., dimensions={0} | all-to-all | bytes 1179648 | tf_op jit(solution)/shard_map/all_to_all | solution.py:405
  81.7 1.8 %combine.1 = bf16[128,640]{1,0:T(8,128)(2,1)} custom-call(bf16[2,8,144,128]{3,2,1,0:T(8,128)(2,1)} %bitcast.9), custom_call_target="tpu_custom_call" | custom-call | tf_op jit(solution)/shard_map/combine/pallas_call | solution.py:69
  (2 shorter events, 0.1 us)
Async XLA Ops:
  29.8 16.2 %collective-permute-start = (bf16[8,256,128]{2,1,0:T(8,128)(2,1)S(1)}, bf16[8,256,128]{2,1,0:T(8,128)(2,1)S(1)}, u32[]{:S(2)}, u32[]{:S(2)}) collective-permute-start(bf16[8,256,128]{2,1,0:T(8,128)(2,1)S(1)} %slice.8.own_ref), channel_id=1, source_target_pairs={{0,24},{8,16},{16,8},{24,0},{32,56},{40,48},{48,40},{56,32},{64,88... | collective-permute-start | bytes 1572872 | tf_op jit(solution)/shard_map/ppermute | solution.py:397
  34.6 11.4 %collective-permute-start.1 = (bf16[8,128,128]{2,1,0:T(8,128)(2,1)S(1)}, bf16[8,128,128]{2,1,0:T(8,128)(2,1)S(1)}, u32[]{:S(2)}, u32[]{:S(2)}) collective-permute-start(bf16[8,128,128]{2,1,0:T(8,128)(2,1)S(1)} %slice.9.q_own_ref), channel_id=1, source_target_pairs={{0,8},{8,0},{16,24},{24,16},{32,40},{40,32},{48,56},{56,48},{64,72... | collective-permute-start | bytes 786440 | tf_op jit(solution)/shard_map/ppermute | solution.py:398
  38.4 0.7 copy-start
  39.1 13.6 %collective-permute-start.2 = (bf16[8,256,128]{2,1,0:T(8,128)(2,1)S(1)}, bf16[8,256,128]{2,1,0:T(8,128)(2,1)S(1)}, u32[]{:S(2)}, u32[]{:S(2)}) collective-permute-start(bf16[8,256,128]{2,1,0:T(8,128)(2,1)S(1)} %slice.8.own_ref), channel_id=1, source_target_pairs={{0,256},{8,264},{16,272},{24,280},{32,288},{40,296},{48,304},{56,3... | collective-permute-start | bytes 1572872 | tf_op jit(solution)/shard_map/ppermute | solution.py:399
  46.0 10.7 %collective-permute-start.3 = (bf16[8,256,128]{2,1,0:T(8,128)(2,1)S(1)}, bf16[8,256,128]{2,1,0:T(8,128)(2,1)S(1)}, u32[]{:S(2)}, u32[]{:S(2)}) collective-permute-start(bf16[8,256,128]{2,1,0:T(8,128)(2,1)S(1)} %slice.8.own_ref), channel_id=1, source_target_pairs={{0,264},{8,256},{16,280},{24,272},{32,296},{40,288},{48,312},{56,3... | collective-permute-start | bytes 1572872 | tf_op jit(solution)/shard_map/ppermute | solution.py:401

commit v8 on v6

--- a/solution.py
+++ b/solution.py
@@ -27,12 +27,12 @@
 LOG2E = math.log2(math.e)
 C = LOG2E / math.sqrt(HEAD_DIM)
 CHIPS = X * Y
-KEY_PAIRS = [(n, n ^ (1 if n >= CHIPS else 3)) for n in range(2 * CHIPS)]
-QUERY_PAIRS = [(n, n ^ (3 if n >= CHIPS else 1)) for n in range(2 * CHIPS)]
+KEY_PAIRS = [(n, n ^ (3 if n >= CHIPS else 1)) for n in range(2 * CHIPS)]
+QUERY_PAIRS = [(n, n ^ (1 if n >= CHIPS else 3)) for n in range(2 * CHIPS)]
 PREV_OWN = [(n, CHIPS + n) for n in range(CHIPS)]
-PREV_PAIR = [(n, CHIPS + (n ^ 1)) for n in range(CHIPS)]
+PREV_PAIR = [(n, CHIPS + (n ^ 3)) for n in range(CHIPS)]
 COLUMNS = [[g * CHIPS + y * X + x for y in range(Y)] for g in range(2) for x in range(X)]
-COLUMN_PAIRS = [COLUMNS[a] + COLUMNS[b] for a, b in ((0, 1), (2, 3), (4, 7), (5, 6))]
+COLUMN_PAIRS = [COLUMNS[a] + COLUMNS[b] for a, b in ((0, 3), (1, 2), (4, 5), (6, 7))]
 
 
 def pack_kernel(q_ref, k_ref, v_ref, out_ref):
@@ -388,8 +388,8 @@
     chip = lax.axis_index("tokens")
     blk, x, y = chip // CHIPS, chip % X, chip // X % Y
     first = blk == 0
-    pairs = [jnp.where(first, x ^ 1, x ^ 3), jnp.where(first, x ^ 3, x ^ 1)]
-    place = jnp.stack([blk, x, y, *pairs, jnp.where(first, x & 1, x // 2)]).astype(jnp.int32)
+    pairs = [jnp.where(first, x ^ 3, x ^ 1), jnp.where(first, x ^ 1, x ^ 3)]
+    place = jnp.stack([blk, x, y, *pairs, jnp.where(first, x // 2, x & 1)]).astype(jnp.int32)
     ints = jnp.concatenate([place, lengths])
     packed = pack(queries, keys, values)
     got = lax.all_to_all(packed, "tokens", 0, 0, tiled=True, axis_index_groups=COLUMNS)

time: 81 us -> 80.8 us (level)
  blocking collectives: 47.4 us -> 43.7 us
  waiting for transfers between devices: 8.32 us -> 10.1 us
    all_to_all x1, blocking collectives: 19.8 us -> 16.1 us  [body(): lax.all_to_all(parts, 'tokens', 0, 0, tiled=True, axis_index_groups=COLUM...]
    ppermute x1, starting transfers between devices: 1.92 us -> 3.72 us  [body(): pair = lax.ppermute(own, 'tokens', KEY_PAIRS)]
    ppermute x1, waiting for transfers between devices: 2.16 us -> 3.56 us  [body(): prev_pair = lax.ppermute(later, 'tokens', PREV_PAIR)]
    ppermute x1, starting transfers between devices: 6.03 us -> 4.77 us  [body(): pair_queries = lax.ppermute(own_queries, 'tokens', QUERY_PAIRS)]
  transfers between devices with their start and end apart: 4 -> 4, of which waited for: 2 -> 2; matrix products, arithmetic and copies ran while one was open for 0% -> 0% of each run, Pallas kernels for 5% -> 6%
where the time goes in v8:
time: 80.8 us; the launch traced here: 80.3 us
  blocking collectives  43.7 us (54%)
  Pallas kernels  14.4 us (18%)
  starting transfers between devices  11.1 us (14%)
  waiting for transfers between devices  10.1 us (12%)
    all_to_all x1, blocking collectives, body(): lax.all_to_all(packed, 'tokens', 0, 0, tiled=True, axis_index_groups=COLU...  27.6 us
    all_to_all x1, blocking collectives, body(): lax.all_to_all(parts, 'tokens', 0, 0, tiled=True, axis_index_groups=COLUM...  16.1 us
    ppermute x1, waiting for transfers between devices, body(): pair = lax.ppermute(own, 'tokens', KEY_PAIRS)  6.54 us
    pallas_call x1, Pallas kernels, attend_prev(): pl.pallas_call(prev_kernel, out_shape=jax.ShapeDtypeStruct((2, Y, ROWS +...  5.79 us
    ppermute x1, starting transfers between devices, body(): pair_queries = lax.ppermute(own_queries, 'tokens', QUERY_PAIRS)  4.77 us
    pallas_call x1, Pallas kernels, attend_own(): pl.pallas_call(own_kernel, out_shape=(jax.ShapeDtypeStruct(ACC, jnp.float...  4.71 us
    ppermute x1, starting transfers between devices, body(): pair = lax.ppermute(own, 'tokens', KEY_PAIRS)  3.72 us
    ppermute x1, waiting for transfers between devices, body(): prev_pair = lax.ppermute(later, 'tokens', PREV_PAIR)  3.56 us
  transfers between devices with their start and end apart: 4, of which 2 were waited for; matrix products, arithmetic and copies ran while one was open for 0% of the time, Pallas kernels for 6%

profile of v8, /device:TPU:1, one launch (start us, length us, event | category | flops | bytes accessed | tf_op | source)
XLA Modules:
  0.0 80.3 jit_solution(10487119195372602739)
XLA Ops:
  0.0 2.1 %pack.1 = bf16[8,384,128]{2,1,0:T(8,128)(2,1)} custom-call(bf16[128,640]{1,0:T(8,128)(2,1)} %q_ref.1, bf16[128,640]{1,0:T(8,128)(2,1)} %k_ref.1, bf16[128,640]{1,0:T(8,128)(2,1)} %v_ref.1), custom_call_target="tpu_custom_call" | custom-call | tf_op jit(solution)/shard_map/pack/pallas_call | solution.py:47
  2.1 27.6 %all_to_all.10 = bf16[8,384,128]{2,1,0:T(8,128)(2,1)S(1)} all-to-all(bf16[8,384,128]{2,1,0:T(8,128)(2,1)} %pack.1), channel_id=1, replica_groups={{0,32,64,96,128,160,192,224},{8,40,72,104,136,168,200,232},{16,48,80,11..., dimensions={0} | all-to-all | bytes 1572864 | tf_op jit(solution)/shard_map/all_to_all | solution.py:395
  29.7 4.8 %collective-permute-start = (bf16[8,128,128]{2,1,0:T(8,128)(2,1)S(1)}, bf16[8,128,128]{2,1,0:T(8,128)(2,1)S(1)}, u32[]{:S(2)}, u32[]{:S(2)}) collective-permute-start(bf16[8,128,128]{2,1,0:T(8,128)(2,1)S(1)} %slice.9.q_own_ref), channel_id=1, source_target_pairs={{0,24},{8,16},{16,8},{24,0},{32,56},{40,48},{48,40},{56,32},{64,88... | collective-permute-start | bytes 786440 | tf_op jit(solution)/shard_map/ppermute | solution.py:398
  34.6 3.7 %collective-permute-start.3 = (bf16[8,256,128]{2,1,0:T(8,128)(2,1)S(1)}, bf16[8,256,128]{2,1,0:T(8,128)(2,1)S(1)}, u32[]{:S(2)}, u32[]{:S(2)}) collective-permute-start(bf16[8,256,128]{2,1,0:T(8,128)(2,1)S(1)} %slice.8.own_ref), channel_id=1, source_target_pairs={{0,8},{8,0},{16,24},{24,16},{32,40},{40,32},{48,56},{56,48},{64,72... | collective-permute-start | bytes 1572872 | tf_op jit(solution)/shard_map/ppermute | solution.py:397
  38.4 0.0 copy-start
  38.4 0.6 copy-done
  39.0 0.1 concatenate.3.int_ref
  39.1 1.3 %collective-permute-start.1 = (bf16[8,256,128]{2,1,0:T(8,128)(2,1)S(1)}, bf16[8,256,128]{2,1,0:T(8,128)(2,1)S(1)}, u32[]{:S(2)}, u32[]{:S(2)}) collective-permute-start(bf16[8,256,128]{2,1,0:T(8,128)(2,1)S(1)} %slice.8.own_ref), channel_id=1, source_target_pairs={{0,256},{8,264},{16,272},{24,280},{32,288},{40,296},{48,304},{56,3... | collective-permute-start | bytes 1572872 | tf_op jit(solution)/shard_map/ppermute | solution.py:399
  40.4 0.0 collective-permute-done.q_pair_ref
  40.4 1.3 %collective-permute-start.2 = (bf16[8,256,128]{2,1,0:T(8,128)(2,1)S(1)}, bf16[8,256,128]{2,1,0:T(8,128)(2,1)S(1)}, u32[]{:S(2)}, u32[]{:S(2)}) collective-permute-start(bf16[8,256,128]{2,1,0:T(8,128)(2,1)S(1)} %slice.8.own_ref), channel_id=1, source_target_pairs={{0,280},{8,272},{16,264},{24,256},{32,312},{40,304},{48,296},{56,2... | collective-permute-start | bytes 1572872 | tf_op jit(solution)/shard_map/ppermute | solution.py:401
  41.7 6.5 %collective-permute-done.3.pair_ref = bf16[8,256,128]{2,1,0:T(8,128)(2,1)S(1)} collective-permute-done((bf16[8,256,128]{2,1,0:T(8,128)(2,1)S(1)}, bf16[8,256,128]{2,1,0:T(8,128)(2,1)S(1)}, u32[]{:S(2)}, u32[]{:S(2)}) %collective-permute-start.3) | collective-permute-done | bytes 524320 | tf_op jit(solution)/shard_map/ppermute | solution.py:397
  48.2 4.7 %attend_own.1 = (f32[4,128,512]{2,1,0:T(8,128)S(1)}, f32[4,8,512]{2,1,0:T(8,128)S(1)}) custom-call(s32[38]{0:T(128)S(1)} %concatenate.3.int_ref, bf16[8,128,128]{2,1,0:T(8,128)(2,1)S(1)} %slice.9.q_own_ref, bf16[8,128,128]{2,1,0:T(8,128)(2,1)S(1)} %collective-permute-done.q_pair_ref, bf16[8,256,128]{2,1,0:T(8,128)(2,1)S(1)} %slice.8.own_ref, ...), custom_call_target="tpu_custom_call" | custom-call | flops 1073741824 | bytes 4194304 | tf_op jit(solution)/shard_map/attend_own/pallas_call | solution.py:355
  53.0 0.0 collective-permute-done.1.prev_own_ref
  53.0 3.6 %collective-permute-done.2.prev_pair_ref = bf16[8,256,128]{2,1,0:T(8,128)(2,1)S(1)} collective-permute-done((bf16[8,256,128]{2,1,0:T(8,128)(2,1)S(1)}, bf16[8,256,128]{2,1,0:T(8,128)(2,1)S(1)}, u32[]{:S(2)}, u32[]{:S(2)}) %collective-permute-start.2) | collective-permute-done | bytes 524320 | tf_op jit(solution)/shard_map/ppermute | solution.py:401
  56.5 5.8 %attend_prev.1 = bf16[2,8,144,128]{3,2,1,0:T(8,128)(2,1)S(1)} custom-call(s32[38]{0:T(128)S(1)} %concatenate.3.int_ref, bf16[8,128,128]{2,1,0:T(8,128)(2,1)S(1)} %slice.9.q_own_ref, bf16[8,128,128]{2,1,0:T(8,128)(2,1)S(1)} %collective-permute-done.q_pair_ref, bf16[8,256,128]{2,1,0:T(8,128)(2,1)S(1)} %collective-permute-done.1.prev_own_ref, ...), custom_call_target="tpu_custom_call" | custom-call | flops 536870912 | bytes 4194304 | tf_op jit(solution)/shard_map/attend_prev/pallas_call | solution.py:373
  62.3 16.1 %all_to_all.11 = bf16[16,144,128]{2,1,0:T(8,128)(2,1)} all-to-all(bf16[16,144,128]{2,1,0:T(8,128)(2,1)S(1)} %bitcast.8), channel_id=1, replica_groups={{0,32,64,96,128,160,192,224,24,56,88,120,152,184,216,248},{8,40,72,104,..., dimensions={0} | all-to-all | bytes 1179648 | tf_op jit(solution)/shard_map/all_to_all | solution.py:405
  78.4 1.8 %combine.1 = bf16[128,640]{1,0:T(8,128)(2,1)} custom-call(bf16[2,8,144,128]{3,2,1,0:T(8,128)(2,1)} %bitcast.9), custom_call_target="tpu_custom_call" | custom-call | tf_op jit(solution)/shard_map/combine/pallas_call | solution.py:69
  (2 shorter events, 0.1 us)
Async XLA Ops:
  29.7 10.7 %collective-permute-start = (bf16[8,128,128]{2,1,0:T(8,128)(2,1)S(1)}, bf16[8,128,128]{2,1,0:T(8,128)(2,1)S(1)}, u32[]{:S(2)}, u32[]{:S(2)}) collective-permute-start(bf16[8,128,128]{2,1,0:T(8,128)(2,1)S(1)} %slice.9.q_own_ref), channel_id=1, source_target_pairs={{0,24},{8,16},{16,8},{24,0},{32,56},{40,48},{48,40},{56,32},{64,88... | collective-permute-start | bytes 786440 | tf_op jit(solution)/shard_map/ppermute | solution.py:398
  34.6 13.7 %collective-permute-start.3 = (bf16[8,256,128]{2,1,0:T(8,128)(2,1)S(1)}, bf16[8,256,128]{2,1,0:T(8,128)(2,1)S(1)}, u32[]{:S(2)}, u32[]{:S(2)}) collective-permute-start(bf16[8,256,128]{2,1,0:T(8,128)(2,1)S(1)} %slice.8.own_ref), channel_id=1, source_target_pairs={{0,8},{8,0},{16,24},{24,16},{32,40},{40,32},{48,56},{56,48},{64,72... | collective-permute-start | bytes 1572872 | tf_op jit(solution)/shard_map/ppermute | solution.py:397
  38.4 0.7 copy-start
  39.1 13.9 %collective-permute-start.1 = (bf16[8,256,128]{2,1,0:T(8,128)(2,1)S(1)}, bf16[8,256,128]{2,1,0:T(8,128)(2,1)S(1)}, u32[]{:S(2)}, u32[]{:S(2)}) collective-permute-start(bf16[8,256,128]{2,1,0:T(8,128)(2,1)S(1)} %slice.8.own_ref), channel_id=1, source_target_pairs={{0,256},{8,264},{16,272},{24,280},{32,288},{40,296},{48,304},{56,3... | collective-permute-start | bytes 1572872 | tf_op jit(solution)/shard_map/ppermute | solution.py:399
  40.4 16.1 %collective-permute-start.2 = (bf16[8,256,128]{2,1,0:T(8,128)(2,1)S(1)}, bf16[8,256,128]{2,1,0:T(8,128)(2,1)S(1)}, u32[]{:S(2)}, u32[]{:S(2)}) collective-permute-start(bf16[8,256,128]{2,1,0:T(8,128)(2,1)S(1)} %slice.8.own_ref), channel_id=1, source_target_pairs={{0,280},{8,272},{16,264},{24,256},{32,312},{40,304},{48,296},{56,2... | collective-permute-start | bytes 1572872 | tf_op jit(solution)/shard_map/ppermute | solution.py:401
